TPU v7x, 256 devices: a whole 4x4x8 slice. The times are simulated.
256 devices in a mesh: dom: 64 (over y, z, core), tile: 4 (over x).
Axes of the slice: x: 4, y: 4, z: 8, core: 2. Of those that a mesh axis runs over, the one named last changes fastest.
Arguments:
- tile_latent: bfloat16 [32768, 512], P(('dom', 'tile')), may hold values from -6 to 6
- relay_pick: int32 [256, 128], P(('dom', 'tile')), may hold values from 0 to 127, as said below
- relay_from: int32 [32768], P(('dom', 'tile')), may hold values from 0 to 255, as said below
- cut_pick: int32 [256, 32], P(('dom', 'tile')), may hold values from 0 to 127, as said below
- edge_latent: bfloat16 [196608, 512], P(('dom', 'tile')), may hold values from -6 to 6
- edge_sender: int32 [196608], P(('dom', 'tile')), may hold values from 0 to 543, as said below
- edge_receiver: int32 [196608], P(('dom', 'tile')), may hold values from 0 to 127, as said below
- edge_in: bfloat16 [1536, 512], replicated, may hold values from -0.15625 to 0.15625
- edge_out: bfloat16 [512, 512], replicated
- node_in: bfloat16 [1024, 512], replicated, may hold values from -0.1875 to 0.1875
- node_out: bfloat16 [512, 512], replicated
- node_cot: bfloat16 [32768, 512], P(('dom', 'tile')), may hold values from -6 to 6
- edge_cot: bfloat16 [196608, 512], P(('dom', 'tile')), may hold values from -6 to 6
Outputs:
- node_update: bfloat16 [32768, 512], P(('dom', 'tile'))
- edge_update: bfloat16 [196608, 512], P(('dom', 'tile'))
- latent_grad: bfloat16 [32768, 512], P(('dom', 'tile'))
- edge_grad: bfloat16 [196608, 512], P(('dom', 'tile'))
- weight_grad: float32 [3584, 512], P('dom', 'tile')
Inputs may be any that keep to these rules, and one draw needn't show every extreme that they name: `relay_pick`: slot j of the block for partition q on device (p, t) carries a row when j is under that pair's count; the counts depend on the partition offset q - p and are 2 or half of it, zero for q = p; the other slots name rows that no one reads. No tile row goes out twice, and the rows that go out nowhere stay on their device. `relay_from`: each device's block names 128 distinct places: its own staying tile rows (below 128) or received slots that carry a row, 128 + s * 2 + j for slot j from partition s. `cut_pick`: distinct rows within a device. `edge_sender`: below 512: a node of the device's own partition; above: a halo slot, first the 16 from the lower partition, then the 16 from the upper. `edge_receiver`: not falling within a device.
All inputs are finite; a program needn't handle non-finite values.
Results may differ from a plain program's by a relative error of at most 0.013.
Values may be sent and summed in bfloat16 or wider, within the bound.
A program may use at most 128 MiB of HBM per device.

v0:
```python
import jax
import jax.numpy as jnp
from jax import lax
from jax.sharding import PartitionSpec as P

EPSILON = 1e-05


def extended(cells, sides, width):
    for axis, dim in sides:
        count = lax.axis_size(axis)
        head = lax.slice_in_dim(cells, 0, width, axis=dim)
        tail = lax.slice_in_dim(cells, cells.shape[dim] - width, cells.shape[dim], axis=dim)
        cells = jnp.concatenate(
            [
                lax.ppermute(tail, axis, [(i, (i + 1) % count) for i in range(count)]),
                cells,
                lax.ppermute(head, axis, [((i + 1) % count, i) for i in range(count)]),
            ],
            axis=dim,
        )
    return cells


def layer_norm(values):
    center = values - jnp.mean(values, -1, keepdims=True)
    inverse = lax.rsqrt(jnp.mean(center * center, -1, keepdims=True) + EPSILON)
    return (center * inverse, inverse)


def norm_grad(normed, inverse, upstream):
    mean_up = jnp.mean(upstream, -1, keepdims=True)
    mean_cross = jnp.mean(upstream * normed, -1, keepdims=True)
    return inverse * (upstream - mean_up - normed * mean_cross)


def silu_grad(values):
    sigmoid = jax.nn.sigmoid(values)
    return sigmoid * (1.0 + values * (1.0 - sigmoid))


def flat_dot(left_mat, right_mat):
    return jnp.dot(left_mat, right_mat, preferred_element_type=jnp.float32)


def inner_dot(left_mat, right_mat):
    return lax.dot_general(
        left_mat, right_mat, (((0,), (0,)), ((), ())), preferred_element_type=jnp.float32
    )


def outer_dot(left_mat, right_mat):
    return lax.dot_general(
        left_mat, right_mat, (((1,), (1,)), ((), ())), preferred_element_type=jnp.float32
    )


def split_parts(values):
    high_part = values.astype(jnp.bfloat16)
    low_part = (values - high_part.astype(jnp.float32)).astype(jnp.bfloat16)
    return (high_part, low_part)


def split_sum(onehot, values):
    high_part, low_part = split_parts(values)
    return inner_dot(onehot, high_part) + inner_dot(onehot, low_part)


def body(
    tile_latent,
    relay_pick,
    relay_from,
    cut_pick,
    edge_latent,
    edge_sender,
    edge_receiver,
    edge_in,
    edge_out,
    node_in,
    node_out,
    node_cot,
    edge_cot,
):
    feat_dim = edge_out.shape[0]
    node_count = tile_latent.shape[0]
    dom_count = lax.axis_size("dom")
    part_count = lax.axis_size("tile") * node_count
    slot_count = relay_pick.shape[1] // dom_count
    halo_rows = cut_pick.shape[1] // 2
    pick_list = relay_pick[0]
    cut_list = cut_pick[0]
    w_edge = edge_in[:feat_dim]
    w_send = edge_in[feat_dim : 2 * feat_dim]
    w_recv = edge_in[2 * feat_dim :]
    w_node = node_in[:feat_dim]
    w_agg = node_in[feat_dim:]
    outgoing = jnp.take(tile_latent, pick_list, axis=0).reshape(dom_count, slot_count, feat_dim)
    incoming = lax.all_to_all(outgoing, "dom", split_axis=0, concat_axis=0, tiled=True)
    pooled = jnp.concatenate([tile_latent, incoming.reshape(dom_count * slot_count, feat_dim)], 0)
    latent = jnp.take(pooled, relay_from, axis=0)
    part_rows = lax.all_gather(latent, "tile", axis=0, tiled=True)
    cut_rows = jnp.take(latent, cut_list, axis=0).reshape(2, halo_rows, feat_dim)
    rim_rows = extended(cut_rows, (("dom", 0),), 1)
    row_table = jnp.concatenate([part_rows, rim_rows[0], rim_rows[3]], 0)
    send_rows = jnp.take(row_table, edge_sender, axis=0)
    send_term = flat_dot(send_rows, w_send)
    recv_rows = jnp.take(latent, edge_receiver, axis=0)
    recv_proj = flat_dot(latent, w_recv)
    edge_pre = (
        flat_dot(edge_latent, w_edge) + send_term + jnp.take(recv_proj, edge_receiver, axis=0)
    )
    edge_act = jax.nn.silu(edge_pre).astype(jnp.bfloat16)
    edge_lin = flat_dot(edge_act, edge_out)
    edge_normed, edge_inv = layer_norm(edge_lin)
    edge_new = (edge_latent.astype(jnp.float32) + edge_normed).astype(jnp.bfloat16)
    incidence = (edge_receiver[:, None] == jnp.arange(node_count, dtype=jnp.int32)[None, :]).astype(
        jnp.bfloat16
    )
    aggregate = inner_dot(incidence, edge_new).astype(jnp.bfloat16)
    node_pre = flat_dot(latent, w_node) + flat_dot(aggregate, w_agg)
    node_act = jax.nn.silu(node_pre).astype(jnp.bfloat16)
    node_lin = flat_dot(node_act, node_out)
    node_normed, node_inv = layer_norm(node_lin)
    node_new = (latent.astype(jnp.float32) + node_normed).astype(jnp.bfloat16)
    node_upstream = node_cot.astype(jnp.float32)
    node_lin_grad = norm_grad(node_normed, node_inv, node_upstream).astype(jnp.bfloat16)
    grad_node_out = inner_dot(node_act, node_lin_grad)
    node_pre_grad = (outer_dot(node_lin_grad, node_out) * silu_grad(node_pre)).astype(jnp.bfloat16)
    grad_node_in = jnp.concatenate(
        [inner_dot(latent, node_pre_grad), inner_dot(aggregate, node_pre_grad)], 0
    )
    node_direct = node_upstream + outer_dot(node_pre_grad, w_node)
    agg_grad = outer_dot(node_pre_grad, w_agg)
    edge_up = edge_cot.astype(jnp.float32) + jnp.take(agg_grad, edge_receiver, axis=0)
    edge_lin_grad = norm_grad(edge_normed, edge_inv, edge_up).astype(jnp.bfloat16)
    grad_edge_out = inner_dot(edge_act, edge_lin_grad)
    edge_pre_grad = (outer_dot(edge_lin_grad, edge_out) * silu_grad(edge_pre)).astype(jnp.bfloat16)
    edge_grad = (edge_up + outer_dot(edge_pre_grad, w_edge)).astype(jnp.bfloat16)
    recv_grad = split_sum(incidence, outer_dot(edge_pre_grad, w_recv))
    node_local = node_direct + recv_grad
    table_rows = part_count + 2 * halo_rows
    sender_onehot = (
        edge_sender[:, None] == jnp.arange(table_rows, dtype=jnp.int32)[None, :]
    ).astype(jnp.bfloat16)
    table_grad = split_sum(sender_onehot, outer_dot(edge_pre_grad, w_send))
    own_grad = lax.psum_scatter(table_grad[:part_count], "tile", scatter_dimension=0, tiled=True)
    rim_grad = extended(
        table_grad[part_count:].reshape(2, halo_rows, feat_dim).astype(jnp.bfloat16),
        (("dom", 0),),
        1,
    ).astype(jnp.float32)
    node_total = (
        node_local
        + own_grad
        + jax.ops.segment_sum(jnp.concatenate([rim_grad[0], rim_grad[3]], 0), cut_list, node_count)
    )
    send_weight = inner_dot(send_rows, edge_pre_grad)
    node_grad = node_total.astype(jnp.bfloat16)
    pool_grad = (
        jnp.zeros((node_count + dom_count * slot_count, feat_dim), jnp.bfloat16)
        .at[relay_from]
        .set(node_grad)
    )
    slot_back = lax.all_to_all(
        pool_grad[node_count:].reshape(dom_count, slot_count, feat_dim),
        "dom",
        split_axis=0,
        concat_axis=0,
        tiled=True,
    )
    latent_grad = (
        pool_grad[:node_count]
        .at[pick_list]
        .add(slot_back.reshape(dom_count * slot_count, feat_dim))
    )
    grad_edge_in = jnp.concatenate(
        [inner_dot(edge_latent, edge_pre_grad), send_weight, inner_dot(recv_rows, edge_pre_grad)], 0
    )
    weight_terms = jnp.concatenate([grad_edge_in, grad_edge_out, grad_node_in, grad_node_out], 0)
    by_rows = lax.psum_scatter(weight_terms, "dom", scatter_dimension=0, tiled=True)
    weight_shard = lax.psum_scatter(by_rows, "tile", scatter_dimension=1, tiled=True)
    return (node_new, edge_new, latent_grad, edge_grad, weight_shard)


def solution(mesh):
    in_specs = (
        P(("dom", "tile"), None),
        P(("dom", "tile"), None),
        P(("dom", "tile")),
        P(("dom", "tile"), None),
        P(("dom", "tile"), None),
        P(("dom", "tile")),
        P(("dom", "tile")),
        P(),
        P(),
        P(),
        P(),
        P(("dom", "tile"), None),
        P(("dom", "tile"), None),
    )
    out_specs = (
        P(("dom", "tile"), None),
        P(("dom", "tile"), None),
        P(("dom", "tile"), None),
        P(("dom", "tile"), None),
        P("dom", "tile"),
    )
    return jax.shard_map(body, mesh=mesh, in_specs=in_specs, out_specs=out_specs, check_vma=False)
```

profile of v0, /device:TPU:1, one launch (start us, length us, event | category | flops | bytes accessed | tf_op | source)
XLA Modules:
  0.0 291.9 jit_solution(13733583338829976748)
XLA Ops:
  7.2 0.8 fusion.50
  8.0 0.7 fusion.49
  8.7 1.8 gather_fusion
  10.5 0.5 broadcast.177
  11.0 1.3 reduce.3
  12.5 0.9 broadcast_select_fusion.3
  13.4 13.2 %all-to-all-start = ((bf16[64,2,512]{2,1,0:T(2,128)(2,1)}), bf16[64,2,512]{2,1,0:T(2,128)(2,1)S(1)}, u32[]{:S(2)}, u32[]{:S(2)}) async-start(bf16[64,2,512]{2,1,0:T(2,128)(2,1)} %broadcast_select_fusion.3), calls=%async_computation | async-start | bytes 262144 | tf_op jit(solution)/shard_map/all_to_all | solution.py:98
  26.7 2.9 fusion.22
  29.6 1.2 copy.24
  31.1 5.8 %all-to-all-done = bf16[64,2,512]{2,1,0:T(2,128)(2,1)S(1)} async-done(((bf16[64,2,512]{2,1,0:T(2,128)(2,1)}), bf16[64,2,512]{2,1,0:T(2,128)(2,1)S(1)}, u32[]{:S(2)}, u32[]{:S(2)}) %all-to-all-start) | async-done | bytes 131104 | tf_op jit(solution)/shard_map/all_to_all | solution.py:98
  37.0 0.8 gather_fusion.1
  37.9 1.3 fusion.16
  39.5 0.6 gather_fusion.2
  40.2 0.5 collective-permute-start.1
  40.6 1.4 collective-permute-start
  42.0 11.4 %all_gather.3 = bf16[512,512]{1,0:T(8,128)(2,1)S(1)} all-gather(bf16[128,512]{1,0:T(8,128)(2,1)S(1)} %broadcast_select_fusion.4), channel_id=1, replica_groups=mesh['dom'=64,'tile'=4] {'tile'}, dimensions={0}, use_global_device_ids=true | all-gather | bytes 655360 | tf_op jit(solution)/shard_map/all_gather | solution.py:101
  53.4 3.1 %gather_fusion.5 = f32[768,512]{1,0:T(8,128)} fusion(f32[128,512]{1,0:T(8,128)S(1)} %fusion.16, s32[1024]{0:T(1024)S(1)} %get-tuple-element.35), kind=kCustom, calls=%fused_computation.clone | custom fusion | bytes 3148800 | tf_op jit(solution)/shard_map/jit(_take)/gather | solution.py:110
  56.5 2.7 gather_fusion.3
  59.2 2.9 %select_add_fusion.1 = f32[768,512]{1,0:T(8,128)S(1)} fusion(f32[768,512]{1,0:T(8,128)} %gather_fusion.5, f32[768,512]{1,0:T(8,128)} %fusion.22, pred[768]{0:T(1024)(128)(4,1)S(1)} %get-tuple-element.39, bf16[1536,512]{1,0:T(8,128)(2,1)} %param.22, bf16[768,512]{1,0:T(8,128)(2,1)S(1)} %gather_fusion.3, pred[768]{0:T(1024)(128)(4,1)S(1)} %get-tuple-element.40), kind=kOutput, calls=%fused_computation.14 | convolution fusion | flops 404226048 | bytes 6030848 | tf_op jit(solution)/shard_map/dot_general | solution.py:43
  62.2 1.2 copy-done.14
  63.4 0.7 fusion.60
  64.4 1.5 copy-done.11
  66.2 0.6 convolution_convert_fusion
  66.8 0.4 copy-done.9
  67.6 0.3 fusion.61
  68.2 0.9 convert_reduce_fusion
  69.0 0.3 fusion.6
  69.7 3.1 %gather_fusion.6 = f32[768,512]{1,0:T(8,128)} fusion(f32[128,512]{1,0:T(8,128)S(1)} %fusion.11, s32[1024]{0:T(1024)S(1)} %get-tuple-element.35), kind=kCustom, calls=%fused_computation.1.clone | custom fusion | bytes 3148800 | tf_op jit(solution)/shard_map/jit(_take)/gather | solution.py:134
  72.8 1.9 copy.26
  74.7 2.0 fusion.55
  76.7 0.6 multiply_convert_fusion.1
  77.3 0.8 copy-done.15
  78.1 0.9 multiply_convert_fusion
  79.1 1.9 fusion.18
  81.1 0.9 fusion
  82.0 1.8 fusion.62
  83.8 1.0 slice.95
  85.1 3.3 %gather_fusion.4 = bf16[768,512]{1,0:T(8,128)(2,1)} fusion(bf16[128,512]{1,0:T(8,128)(2,1)S(1)} %broadcast_select_fusion.4, s32[1024]{0:T(1024)S(1)} %get-tuple-element.35), kind=kCustom, calls=%fused_computation.6 | custom fusion | bytes 1575936 | tf_op jit(solution)/shard_map/jit(_take)/gather | solution.py:107
  88.4 3.1 %fusion.3 = f32[3584,512]{1,0:T(8,128)} fusion(bf16[768,512]{1,0:T(8,128)(2,1)} %copy-done.5, bf16[768,512]{1,0:T(8,128)(2,1)} %param.19), kind=kOutput, calls=%fused_computation.34 | convolution fusion | flops 402653184 | bytes 2621440 | tf_op jit(solution)/shard_map/dot_general | solution.py:47
  91.6 1.7 convolution_dynamic-update-slice_fusion.2
  93.2 1.7 convolution_dynamic-update-slice_fusion.1
  94.9 0.4 copy-done.20
  95.4 1.6 convolution_dynamic-update-slice_fusion
  97.0 1.3 convolution_dynamic-update-slice_fusion.5
  98.4 1.3 convolution_dynamic-update-slice_fusion.4
  99.7 1.4 convolution_dynamic-update-slice_fusion.3
  101.1 0.7 slice_bitcast_fusion.1
  101.9 1.7 collective-permute-start.3
  103.6 0.4 collective-permute-start.2
  104.0 1.9 fusion.14
  105.9 0.5 fusion.30
  106.4 1.2 convolution_add_fusion
  107.6 2.3 copy.28
  109.9 0.8 slice.97
  110.8 1.5 fusion.5
  112.3 1.0 scatter_custom_fusion
  113.3 1.3 scatter_custom_fusion.1
  114.6 0.7 reshape.164
  115.3 8.7 %all-to-all-start.1 = ((bf16[64,2,512]{2,1,0:T(2,128)(2,1)}), bf16[64,2,512]{2,1,0:T(2,128)(2,1)S(1)}, u32[]{:S(2)}, u32[]{:S(2)}) async-start(bf16[64,2,512]{2,1,0:T(2,128)(2,1)} %reshape.164), calls=%async_computation.2 | async-start | bytes 262144 | tf_op jit(solution)/shard_map/all_to_all | solution.py:164
  124.1 134.0 %reduce-scatter.6.cloned.1.call-done = f32[56,512]{1,0:T(8,128)} async-done(((f32[3584,512]{1,0:T(8,128)}), f32[56,512]{1,0:T(8,128)}) %reduce-scatter.6.cloned.1.call-update) | async-done | bytes 114704 | tf_op jit(solution)/shard_map/reduce_scatter | solution.py:180
  258.2 2.8 add_convert_fusion
  261.0 2.3 copy.29
  263.3 1.5 scatter_fusion
  264.8 20.5 %reduce-scatter.8.cloned.1.call-done = f32[56,128]{1,0:T(8,128)} async-done(((f32[56,512]{1,0:T(8,128)}), f32[56,128]{1,0:T(8,128)}) %reduce-scatter.8.cloned.1.call-update) | async-done | bytes 28688 | tf_op jit(solution)/shard_map/reduce_scatter | solution.py:181
  (139 shorter events, 3.1 us)
Async XLA Ops:
  7.2 56.3 %copy-start = (bf16[512,512]{1,0:T(8,128)(2,1)S(1)}, bf16[512,512]{1,0:T(8,128)(2,1)}, u32[]{:S(2)}) copy-start(bf16[512,512]{1,0:T(8,128)(2,1)} %param.23) | copy-start | bytes 1572868
  7.2 19.5 %copy-start.43 = (s32[1,32]{1,0:T(1,128)S(1)}, s32[1,32]{1,0:T(1,128)}, u32[]{:S(2)}) copy-start(s32[1,32]{1,0:T(1,128)} %param.18) | copy-start | bytes 388
  7.2 19.4 %copy-start.42 = (s32[128]{0:T(128)S(1)}, s32[128]{0:T(128)}, u32[]{:S(2)}) copy-start(s32[128]{0:T(128)} %param.17) | copy-start | bytes 1540
  7.2 19.5 %copy-start.26 = (s32[768]{0:T(1024)S(1)}, s32[768]{0:T(1024)}, u32[]{:S(2)}) copy-start(s32[768]{0:T(1024)} %param.21) | copy-start | bytes 9220
  7.2 19.5 %copy-start.27 = (s32[768]{0:T(1024)S(1)}, s32[768]{0:T(1024)}, u32[]{:S(2)}) copy-start(s32[768]{0:T(1024)} %param.20) | copy-start | bytes 9220
  7.2 19.5 %copy-start.10 = (bf16[768,512]{1,0:T(8,128)(2,1)S(1)}, bf16[768,512]{1,0:T(8,128)(2,1)}, u32[]{:S(2)}) copy-start(bf16[768,512]{1,0:T(8,128)(2,1)} %param.19) | copy-start | bytes 2359300
  8.6 21.0 %copy-start.34 = (s32[128]{0:T(128)}, s32[128]{0:T(128)S(1)}, u32[]{:S(2)}) copy-start(s32[128]{0:T(128)S(1)} %fusion.49) | copy-start | bytes 1540
  13.4 23.5 %all-to-all-start = ((bf16[64,2,512]{2,1,0:T(2,128)(2,1)}), bf16[64,2,512]{2,1,0:T(2,128)(2,1)S(1)}, u32[]{:S(2)}, u32[]{:S(2)}) async-start(bf16[64,2,512]{2,1,0:T(2,128)(2,1)} %broadcast_select_fusion.3), calls=%async_computation | async-start | bytes 262144 | tf_op jit(solution)/shard_map/all_to_all | solution.py:98
  26.5 84.2 %reduce-scatter.4.cloned.1.call-start = ((), (), s32[]{:S(2)}) async-start(), calls=%async_computation.5 | async-start | bytes 1310720 | tf_op jit(solution)/shard_map/reduce_scatter | solution.py:146
  26.6 4.2 %copy-start.38 = (s32[128]{0:T(128)}, s32[128]{0:T(128)S(1)}, u32[]{:S(2)}) copy-start(s32[128]{0:T(128)S(1)} %compare_select_fusion.6) | copy-start | bytes 1540
  26.7 4.1 %copy-start.18 = (bf16[768,512]{1,0:T(8,128)(2,1)S(1)}, bf16[768,512]{1,0:T(8,128)(2,1)}, u32[]{:S(2)}) copy-start(bf16[768,512]{1,0:T(8,128)(2,1)} %param.27) | copy-start | bytes 2359300
  29.6 7.4 %copy-start.4 = (bf16[128,512]{1,0:T(8,128)(2,1)S(1)}, bf16[128,512]{1,0:T(8,128)(2,1)}, u32[]{:S(2)}) copy-start(bf16[128,512]{1,0:T(8,128)(2,1)} %param.15) | copy-start | bytes 393220
  31.1 28.1 %copy-start.29 = (pred[768]{0:T(1024)(128)(4,1)}, pred[768]{0:T(1024)(128)(4,1)S(1)}, u32[]{:S(2)}) copy-start(pred[768]{0:T(1024)(128)(4,1)S(1)} %get-tuple-element.39) | copy-start | bytes 2308
  31.1 28.1 %copy-start.32 = (pred[768]{0:T(1024)(128)(4,1)}, pred[768]{0:T(1024)(128)(4,1)S(1)}, u32[]{:S(2)}) copy-start(pred[768]{0:T(1024)(128)(4,1)S(1)} %get-tuple-element.40) | copy-start | bytes 2308
  31.1 8.1 %copy-start.8 = (bf16[1024,512]{1,0:T(8,128)(2,1)S(1)}, bf16[1024,512]{1,0:T(8,128)(2,1)}, u32[]{:S(2)}) copy-start(bf16[1024,512]{1,0:T(8,128)(2,1)} %param.24) | copy-start | bytes 3145732
  40.2 16.3 %collective-permute-start.1 = (bf16[1,16,512]{2,1,0:T(8,128)(2,1)S(1)}, bf16[1,16,512]{2,1,0:T(8,128)(2,1)S(1)}, u32[]{:S(2)}, u32[]{:S(2)}) collective-permute-start(bf16[1,16,512]{2,1,0:T(8,128)(2,1)S(1)} %get-tuple-element.28), channel_id=1, source_target_pairs={{4,0},{8,4},{12,8},{16,12},{20,16},{24,20},{28,24},{32,28},{36,32}... | collective-permute-start | bytes 49160 | tf_op jit(solution)/shard_map/ppermute | solution.py:18
  40.6 15.8 %collective-permute-start = (bf16[1,16,512]{2,1,0:T(8,128)(2,1)S(1)}, bf16[1,16,512]{2,1,0:T(8,128)(2,1)S(1)}, u32[]{:S(2)}, u32[]{:S(2)}) collective-permute-start(bf16[1,16,512]{2,1,0:T(8,128)(2,1)S(1)} %get-tuple-element.27), channel_id=1, source_target_pairs={{0,4},{4,8},{8,12},{12,16},{16,20},{20,24},{24,28},{28,32},{32,36}... | collective-permute-start | bytes 49160 | tf_op jit(solution)/shard_map/ppermute | solution.py:16
  59.2 3.0 %copy-start.12 = (bf16[768,512]{1,0:T(8,128)(2,1)}, bf16[768,512]{1,0:T(8,128)(2,1)S(1)}, u32[]{:S(2)}) copy-start(bf16[768,512]{1,0:T(8,128)(2,1)S(1)} %gather_fusion.3) | copy-start | bytes 2359300
  62.2 1.2 copy-start.14
  64.2 2.0 copy-start.1
  64.2 1.7 copy-start.11
  65.9 1.3 copy-start.9
  66.1 1.8 copy-start.7
  66.2 1.4 copy-start.41
  67.2 0.9 copy-start.21
  67.6 1.8 copy-start.24
  67.9 1.5 copy-start.36
  68.2 1.2 copy-start.39
  69.0 0.7 copy-start.44
  69.0 0.7 copy-start.46
  74.7 2.0 copy-start.2
  74.7 2.0 copy-start.30
  76.7 1.4 copy-start.15
  78.1 1.0 copy-start.19
  79.1 2.9 copy-start.5
  79.1 2.0 copy-start.28
  84.8 173.3 %reduce-scatter.6.cloned.1.call-start = ((), (), s32[]{:S(2)}) async-start(), calls=%async_computation.6 | async-start | bytes 7454720 | tf_op jit(solution)/shard_map/reduce_scatter | solution.py:180
  88.4 3.1 %copy-start.6 = (bf16[768,512]{1,0:T(8,128)(2,1)S(1)}, bf16[768,512]{1,0:T(8,128)(2,1)}, u32[]{:S(2)}) copy-start(bf16[768,512]{1,0:T(8,128)(2,1)} %copy-done.5) | copy-start | bytes 2359300
  88.4 3.1 %copy-start.13 = (bf16[768,512]{1,0:T(8,128)(2,1)S(1)}, bf16[768,512]{1,0:T(8,128)(2,1)}, u32[]{:S(2)}) copy-start(bf16[768,512]{1,0:T(8,128)(2,1)} %copy-done.12) | copy-start | bytes 2359300
  88.4 3.1 %copy-start.33 = (pred[768]{0:T(1024)(128)(4,1)S(1)}, pred[768]{0:T(1024)(128)(4,1)}, u32[]{:S(2)}) copy-start(pred[768]{0:T(1024)(128)(4,1)} %copy-done.32) | copy-start | bytes 2308
  91.5 1.7 copy-start.17
  91.5 1.7 copy-start.31
  93.2 1.7 copy-start.16
  93.2 2.1 copy-start.20
  97.0 2.7 copy-start.22
  97.0 2.7 copy-start.25
  97.0 2.7 copy-start.37
  97.0 2.7 copy-start.40
  97.0 2.7 copy-start.45
  97.0 2.7 copy-start.47
  101.9 8.9 %collective-permute-start.3 = (bf16[1,16,512]{2,1,0:T(8,128)(2,1)S(1)}, bf16[1,16,512]{2,1,0:T(8,128)(2,1)S(1)}, u32[]{:S(2)}, u32[]{:S(2)}) collective-permute-start(bf16[1,16,512]{2,1,0:T(8,128)(2,1)S(1)} %get-tuple-element.21), channel_id=1, source_target_pairs={{4,0},{8,4},{12,8},{16,12},{20,16},{24,20},{28,24},{32,28},{36,32}... | collective-permute-start | bytes 49160 | tf_op jit(solution)/shard_map/ppermute | solution.py:18
  103.6 7.1 %collective-permute-start.2 = (bf16[1,16,512]{2,1,0:T(8,128)(2,1)S(1)}, bf16[1,16,512]{2,1,0:T(8,128)(2,1)S(1)}, u32[]{:S(2)}, u32[]{:S(2)}) collective-permute-start(bf16[1,16,512]{2,1,0:T(8,128)(2,1)S(1)} %get-tuple-element.20), channel_id=1, source_target_pairs={{0,4},{4,8},{8,12},{12,16},{16,20},{20,24},{24,28},{28,32},{32,36}... | collective-permute-start | bytes 49160 | tf_op jit(solution)/shard_map/ppermute | solution.py:16
  106.4 4.3 %copy-start.23 = (bf16[128,512]{1,0:T(8,128)(2,1)S(1)}, bf16[128,512]{1,0:T(8,128)(2,1)}, u32[]{:S(2)}) copy-start(bf16[128,512]{1,0:T(8,128)(2,1)} %param.26) | copy-start | bytes 393220
  115.3 147.9 %all-to-all-start.1 = ((bf16[64,2,512]{2,1,0:T(2,128)(2,1)}), bf16[64,2,512]{2,1,0:T(2,128)(2,1)S(1)}, u32[]{:S(2)}, u32[]{:S(2)}) async-start(bf16[64,2,512]{2,1,0:T(2,128)(2,1)} %reshape.164), calls=%async_computation.2 | async-start | bytes 262144 | tf_op jit(solution)/shard_map/all_to_all | solution.py:164
  124.1 161.3 %reduce-scatter.8.cloned.1.call-start = ((), (), s32[]{:S(2)}) async-start(), calls=%async_computation.7 | async-start | bytes 143360 | tf_op jit(solution)/shard_map/reduce_scatter | solution.py:181
  261.0 2.4 copy-start.35
  264.8 20.6 %copy-start.3 = (bf16[128,512]{1,0:T(8,128)(2,1)}, bf16[128,512]{1,0:T(8,128)(2,1)S(1)}, u32[]{:S(2)}) copy-start(bf16[128,512]{1,0:T(8,128)(2,1)S(1)} %scatter_fusion) | copy-start | bytes 393220
Sparse Core Ops, SparseCore 0:
  85.0 22.4 reduce-scatter.3
  112.3 145.8 reduce-scatter.5
  261.4 23.9 reduce-scatter.7
where the time goes:
time: 294 us; the launch traced here: 292 us
  waiting for transfers between devices  160 us (54%)
  matrix products  35.4 us (12%)
  local copies, waits for them, and re-layouts  32.2 us (11%)
  starting transfers between devices  26.2 us (9%)
  between operations  14.6 us (5%)
  other arithmetic  11.7 us (4%)
  blocking collectives  11.4 us (4%)
    reduce_scatter x1, waiting for transfers between devices, body(): lax.psum_scatter(weight_terms, 'dom', scatter_dimension=0, tiled=True)  134 us
    reduce_scatter x1, waiting for transfers between devices, body(): lax.psum_scatter(by_rows, 'tile', scatter_dimension=1, tiled=True)  20.5 us
    dot_general x12, matrix products, inner_dot(): lax.dot_general(left_mat, right_mat, (((0,), (0,)), ((), ())), preferred_...  17.1 us
    all_to_all x1, starting transfers between devices, body(): lax.all_to_all(outgoing, 'dom', split_axis=0, concat_axis=0, tiled=True)  13.2 us
    all_gather x1, blocking collectives, body(): part_rows = lax.all_gather(latent, 'tile', axis=0, tiled=True)  11.4 us
    unnamed x101, local copies, waits for them, and re-layouts  11.3 us
    dot_general x7, matrix products, outer_dot(): lax.dot_general(left_mat, right_mat, (((1,), (1,)), ((), ())), preferred_...  9.68 us
    all_to_all x1, starting transfers between devices, body(): lax.all_to_all(pool_grad[node_count:].reshape(dom_count, slot_count, feat...  8.73 us
  transfers between devices with their start and end apart: 9, of which 3 were waited for; matrix products, arithmetic and copies ran while one was open for 14% of the time, Pallas kernels for 0%

commit v1 on v0

v1 whole, which is shorter than its diff:
```python
import jax
import jax.numpy as jnp
from jax import lax
from jax.experimental import pallas as pl
from jax.experimental.pallas import tpu as pltpu
from jax.sharding import PartitionSpec as P

EPSILON = 1e-05
MESH = pl.DeviceIdType.MESH
F32 = jnp.float32
BF16 = jnp.bfloat16
NX, NY, NZ, NC = 4, 4, 8, 2
DOM = NY * NZ * NC
H = 512
ND = 128
ED = 768
EB = 256
TR = 640
LN = 128


def iota(shape, dim):
    return lax.broadcasted_iota(jnp.int32, shape, dim)


def onehot(mask):
    return jnp.where(mask, 1.0, 0.0).astype(BF16)


def dot(a, b):
    return lax.dot_general(a, b, (((1,), (0,)), ((), ())), preferred_element_type=F32)


def dot_nt(a, b):
    return lax.dot_general(a, b, (((1,), (1,)), ((), ())), preferred_element_type=F32)


def dot_tn(a, b):
    return lax.dot_general(a, b, (((0,), (0,)), ((), ())), preferred_element_type=F32)


def norm(v):
    center = v - jnp.mean(v, -1, keepdims=True)
    inv = lax.rsqrt(jnp.mean(center * center, -1, keepdims=True) + EPSILON)
    return center * inv, inv


def norm_grad(normed, inv, up):
    mean_up = jnp.mean(up, -1, keepdims=True)
    mean_cross = jnp.mean(up * normed, -1, keepdims=True)
    return inv * (up - mean_up - normed * mean_cross)


def silu_pair(v):
    sig = 1.0 / (1.0 + jnp.exp(-v))
    act = v * sig
    return act, sig + act * (1.0 - sig)


def hi_lo(v):
    hi = v.astype(BF16)
    return hi, (v - hi.astype(F32)).astype(BF16)


def kernel(
    tile_ref, pick_ref, from_ref, cut_ref, snd_ref, rcv_ref, ncot_ref,
    e_hbm, cot_hbm, ein_hbm, eout_hbm, nin_hbm, nout_hbm,
    nodeup_ref, edgeup_hbm, latgrad_ref, edgegrad_hbm, wgrad_ref,
    e, cot, ein, eout, nin, nout, lsem,
    msg, inc, msgb, incb, table, lat, halo_s,
    sel_s, sel_st, sel_r, sel_rt, gat_i, back_o, back_p,
    pre, act, dsilu, normed, einv, enew, egrad, plg, ppg,
    gsum, gs, gr, hb, wg,
    csend, crecv, chip, rx, bx, ry, ry1, b1, rx1, zown, zp, rz,
    r_s, r_r, a_s, a_r, rb_s, rb_r, g_s, g_r, c_s, c_r, s2_s, s2_r, s3_s, s3_r, z_s, z_r,
):
    p = lax.axis_index("dom")
    x = lax.axis_index("tile")
    core = lax.rem(p, NC)
    z = lax.rem(p // NC, NZ)
    y = p // (NC * NZ)
    up = lax.rem(p + 1, DOM)
    dn = lax.rem(p + DOM - 1, DOM)
    sib = p + 1 - 2 * core

    def xpeer(j):
        return lax.rem(x + j, NX)

    def remote(src, dst, ss, rs, d, t):
        return pltpu.make_async_remote_copy(
            src, dst, ss, rs, device_id=(d, t), device_id_type=MESH
        )

    barrier = pltpu.get_barrier_semaphore()

    def greet(i, carry):
        pl.semaphore_signal(
            barrier, 1, device_id=(lax.rem(p + i, DOM), x), device_id_type=MESH
        )
        return carry

    lax.fori_loop(1, DOM, greet, 0)
    for j in range(1, NX):
        pl.semaphore_signal(barrier, 1, device_id=(p, xpeer(j)), device_id_type=MESH)

    loads = [
        pltpu.make_async_copy(s, d, lsem.at[i])
        for i, (s, d) in enumerate(
            (
                (e_hbm, e), (ein_hbm, ein), (eout_hbm, eout), (nin_hbm, nin),
                (nout_hbm, nout), (cot_hbm, cot),
            )
        )
    ]
    for c in loads:
        c.start()

    pickb = jnp.broadcast_to(pick_ref[...], (ND, LN)).astype(F32).astype(BF16)
    quad = onehot(iota((4 * LN, LN), 0) // 4 == iota((4 * LN, LN), 1))
    rep = dot_nt(quad, pickb)
    qlane = iota((4 * LN, LN), 1).astype(F32)
    qmod = iota((4 * LN, LN), 0) % 4
    out = jnp.zeros((4 * LN, LN), F32)
    for c in range(4):
        out += dot(
            onehot((rep == qlane) & (qmod == c)), tile_ref[:, c * LN : (c + 1) * LN]
        )
    msg[...] = out.reshape(DOM, 8, LN).astype(BF16)
    inc[p] = jnp.zeros((8, LN), BF16)
    incb[p] = jnp.zeros((8, LN), BF16)

    pl.semaphore_wait(barrier, DOM - 1 + NX - 1)

    def relay(i, carry):
        q = lax.rem(p + i, DOM)
        remote(msg.at[q], inc.at[p], r_s, r_r, q, x).start()
        return carry

    lax.fori_loop(1, DOM, relay, 0)

    frow = jnp.broadcast_to(from_ref[...], (LN, ND))
    fcol = frow.T
    fcol4 = jnp.concatenate([fcol] * 4, 1)
    for c in range(4):
        gat_i[c * ND : (c + 1) * ND, :] = onehot(
            (fcol4 - ND) * 4 + c == iota((ND, 4 * LN), 1)
        )
    stay = onehot(fcol == iota((ND, LN), 1))

    lane = iota((LN, LN), 1)
    subl = iota((LN, LN), 0)

    def selections(b, carry):
        rows = pl.ds(pl.multiple_of(b * LN, LN), LN)
        srow = jnp.broadcast_to(snd_ref[pl.ds(b, 1), :], (LN, LN))
        rrow = jnp.broadcast_to(rcv_ref[pl.ds(b, 1), :], (LN, LN))
        scol = srow.T
        rcol = rrow.T
        for k in range(TR // LN):
            sel_s[rows, k * LN : (k + 1) * LN] = onehot(scol == lane + k * LN)
            sel_st[k * LN : (k + 1) * LN, rows] = onehot(srow == subl + k * LN)
        r = onehot(rcol == lane)
        sel_r[rows, :LN] = r
        sel_r[rows, LN:] = r
        sel_rt[:, rows] = onehot(rrow == subl)
        return carry

    lax.fori_loop(0, ED // LN, selections, 0)
    table[pl.ds(NX * ND + 32, TR - NX * ND - 32), :] = jnp.zeros((TR - NX * ND - 32, H), BF16)

    loads[0].wait()
    loads[1].wait()

    def edge_term(b, carry):
        rows = pl.ds(pl.multiple_of(b * EB, EB), EB)
        pre[rows, :] = dot(e[rows, :], ein[:H, :])
        return carry

    lax.fori_loop(0, ED // EB, edge_term, 0)

    pltpu.make_async_copy(inc.at[pl.ds(0, DOM - 1)], inc.at[pl.ds(0, DOM - 1)], r_r).wait()
    got = inc[...].astype(F32).reshape(4 * LN, LN).astype(BF16)
    slots = dot(gat_i[...], got)
    latent = jnp.concatenate(
        [
            (
                dot(stay, tile_ref[:, c * LN : (c + 1) * LN])
                + slots[c * ND : (c + 1) * ND, :]
            ).astype(BF16)
            for c in range(4)
        ],
        1,
    )
    lat[...] = latent
    own_rows = pl.ds(pl.multiple_of(x * ND, ND), ND)
    table[own_rows, :] = latent

    gathers = [
        remote(table.at[own_rows], table.at[own_rows], a_s.at[j], a_r.at[j], p, xpeer(j))
        for j in (1, 3, 2)
    ]
    for c in gathers:
        c.start()
    cutb = jnp.broadcast_to(cut_ref[...], (LN, 32)).astype(F32).astype(BF16)
    eye = onehot(iota((32, 32), 0) == iota((32, 32), 1))
    ccol = dot_nt(eye, cutb)
    halo_s[...] = dot(onehot(ccol == iota((32, LN), 1).astype(F32)), latent).astype(BF16)
    halos = [
        remote(halo_s.at[pl.ds(16, 16)], table.at[pl.ds(512, 16)], a_s.at[0], a_r.at[0], up, x),
        remote(halo_s.at[pl.ds(0, 16)], table.at[pl.ds(528, 16)], a_s.at[4], a_r.at[4], dn, x),
    ]
    for c in halos:
        c.start()

    rh, rl = hi_lo(dot(latent, ein[2 * H :, :]))
    recv_proj = jnp.concatenate([rh, rl], 0)

    def recv_term(b, carry):
        rows = pl.ds(pl.multiple_of(b * EB, EB), EB)
        pre[rows, :] += dot(sel_r[rows, :], recv_proj)
        return carry

    lax.fori_loop(0, ED // EB, recv_term, 0)
    prow = dot_nt(pickb, quad)
    pq = iota((ND, 4 * LN), 1) % 4
    pn = iota((ND, 4 * LN), 0).astype(F32)
    frow4 = jnp.broadcast_to(from_ref[...], (4 * LN, ND))
    fq = iota((4 * LN, ND), 0)
    for c in range(4):
        back_o[c * ND : (c + 1) * ND, :] = onehot((prow == pn) & (pq == c))
        back_p[:, c * ND : (c + 1) * ND] = onehot((frow4 - ND) * 4 + c == fq)
    for c in loads[2:]:
        c.wait()

    for c in gathers:
        c.wait_recv()
    for c in halos:
        c.wait_recv()

    def edge_forward(b, carry):
        rows = pl.ds(pl.multiple_of(b * EB, EB), EB)
        send_rows = dot(sel_s[rows, :], table[...]).astype(BF16)
        a, da = silu_pair(pre[rows, :] + dot(send_rows, ein[H : 2 * H, :]))
        a = a.astype(BF16)
        act[rows, :] = a
        dsilu[rows, :] = da
        yn, inv = norm(dot(a, eout[...]))
        normed[rows, :] = yn
        einv[rows, :] = jnp.broadcast_to(inv, (EB, LN))
        enew[rows, :] = (e[rows, :].astype(F32) + yn).astype(BF16)
        return carry

    lax.fori_loop(0, ED // EB, edge_forward, 0)
    st_new = pltpu.make_async_copy(enew, edgeup_hbm, lsem.at[6])
    st_new.start()

    agg = dot(sel_rt[...], enew[...]).astype(BF16)
    node_act, node_dsilu = silu_pair(dot(latent, nin[:H, :]) + dot(agg, nin[H:, :]))
    node_act = node_act.astype(BF16)
    nnorm, ninv = norm(dot(node_act, nout[...]))
    nodeup_ref[...] = (latent.astype(F32) + nnorm).astype(BF16)
    ncot = ncot_ref[...].astype(F32)
    nlg = norm_grad(nnorm, ninv, ncot).astype(BF16)
    npg = (dot_nt(nlg, nout[...]) * node_dsilu).astype(BF16)
    agh, agl = hi_lo(dot_nt(npg, nin[H:, :]))
    agg_grad = jnp.concatenate([agh, agl], 0)
    node_direct = ncot + dot_nt(npg, nin[:H, :])
    wg[4 * H : 5 * H, :] = dot_tn(latent, npg)
    wg[5 * H : 6 * H, :] = dot_tn(agg, npg)
    wg[6 * H :, :] = dot_tn(node_act, nlg)

    half = 7 * ED // 12

    def two_blocks(block, k, side):
        base = 2 * half * block + 4 * 56 * k + 56 * side
        return jnp.concatenate(
            [
                wg[pl.ds(pl.multiple_of(base, 8), 56), :],
                wg[pl.ds(pl.multiple_of(base + 112, 8), 56), :],
            ],
            0,
        )

    def core_copy(block):
        rows = pl.ds(half * block, half)
        return remote(
            csend.at[rows], crecv.at[rows], c_s.at[block], c_r.at[block], sib, x
        )

    def pack_core(block):
        def body(k, carry):
            rows = pl.ds(pl.multiple_of(half * block + 112 * k, 16), 112)
            csend[rows, :] = two_blocks(block, k, 1 - core).astype(BF16)
            return carry

        lax.fori_loop(0, 4, body, 0)
        core_copy(block).start()

    def x_copy(block, j):
        t = xpeer(j)
        cols = pl.ds(pl.multiple_of(t * LN, LN), LN)
        i = 3 * block + j - 1
        return remote(
            chip.at[pl.ds(half * block, half), cols], rx.at[i], s2_s.at[i], s2_r.at[i], p, t
        )

    def y_index(block):
        return lax.rem(block - y + NY, NY)

    def y_copy(src, dst, ss, rs, block):
        j = y_index(block) - 1
        return remote(src, dst.at[j], ss.at[j], rs.at[j], p + (block - y) * NC * NZ, x)

    def y1_copy(block):
        return y_copy(chip.at[pl.ds(half * block, half)], ry1, s3_s, s3_r, block)

    def y0_copy(block):
        return y_copy(bx.at[block], ry, s3_s, s3_r, block)

    def x1_copy(j):
        t = xpeer(j)
        cols = pl.ds(pl.multiple_of(t * LN, LN), LN)
        return remote(b1.at[:, cols], rx1.at[j - 1], s2_s.at[j - 1], s2_r.at[j - 1], p, t)

    def combine(block):
        core_copy(block).wait_recv()

        def body(k, carry):
            rows = pl.ds(pl.multiple_of(half * block + 112 * k, 16), 112)
            chip[rows, :] = (
                two_blocks(block, k, core) + crecv[rows, :].astype(F32)
            ).astype(BF16)
            return carry

        lax.fori_loop(0, 4, body, 0)

        @pl.when(core == 0)
        def _():
            for j in (1, 3, 2):
                x_copy(block, j).start()

        @pl.when((core == 1) & (y != block))
        def _():
            y1_copy(block).start()

    pack_core(3)

    def edge_backward(b, carry):
        rows = pl.ds(pl.multiple_of(b * EB, EB), EB)
        upst = cot[rows, :].astype(F32) + dot(sel_r[rows, :], agg_grad)
        g = norm_grad(normed[rows, :], einv[rows, :1], upst).astype(BF16)
        plg[rows, :] = g
        pg = (dot_nt(g, eout[...]) * dsilu[rows, :]).astype(BF16)
        ppg[rows, :] = pg
        egrad[rows, :] = (upst + dot_nt(pg, ein[:H, :])).astype(BF16)
        return carry

    lax.fori_loop(0, ED // EB, edge_backward, 0)
    gsum[...] = dot(sel_st[...], ppg[...])
    gs[...] = gsum[...].astype(BF16)

    def own_of(t):
        return pl.ds(pl.multiple_of(t * ND, ND), ND)

    scatters = [
        remote(gs.at[own_of(xpeer(j))], gr.at[j - 1], g_s.at[j], g_r.at[j], p, xpeer(j))
        for j in (1, 3, 2)
    ] + [
        remote(gs.at[pl.ds(512, 16)], hb.at[pl.ds(16, 16)], g_s.at[0], g_r.at[0], dn, x),
        remote(gs.at[pl.ds(528, 16)], hb.at[pl.ds(0, 16)], g_s.at[4], g_r.at[4], up, x),
    ]
    for c in scatters:
        c.start()
    st_grad = pltpu.make_async_copy(egrad, edgegrad_hbm, lsem.at[7])
    st_grad.start()
    combine(3)
    wg[3 * H : 4 * H, :] = dot_tn(act[...], plg[...])
    pack_core(2)
    grecv = dot(sel_rt[...], ppg[...]).astype(BF16)
    node_part = node_direct + dot_nt(grecv, ein[2 * H :, :])
    wg[2 * H : 3 * H, :] = dot_tn(latent, grecv)
    wg[H : 2 * H, :] = dot_tn(table[...], gs[...])
    pack_core(1)
    combine(2)
    wg[:H, :] = dot_tn(e[...], ppg[...])
    pack_core(0)
    combine(1)

    for c in scatters:
        c.wait_recv()
    crow = jnp.broadcast_to(cut_ref[...], (ND, 32))
    total = dot(onehot(crow == iota((ND, 32), 0)), hb[...])
    total += gsum[own_rows, :]
    for j in range(3):
        total += gr[j].astype(F32)
    node_grad = (node_part + dot_nt(total.astype(BF16), ein[H : 2 * H, :])).astype(BF16)
    ng = jnp.concatenate([node_grad[:, c * LN : (c + 1) * LN] for c in range(4)], 0)
    msgb[...] = dot(back_p[...], ng).reshape(DOM, 8, LN).astype(BF16)

    def relay_back(i, carry):
        q = lax.rem(p + i, DOM)
        remote(msgb.at[q], incb.at[p], rb_s, rb_r, q, x).start()
        return carry

    lax.fori_loop(1, DOM, relay_back, 0)
    combine(0)

    mine = pl.ds(pl.multiple_of(x * LN, LN), LN)

    @pl.when(core == 0)
    def _():
        for block in (3, 2, 1, 0):
            total = chip[pl.ds(half * block, half), mine].astype(F32)
            for j in (1, 3, 2):
                x_copy(block, j).wait_recv()
                total += rx[3 * block + j - 1].astype(F32)
            bx[block] = total.astype(BF16)

            @pl.when(y != block)
            def _():
                y0_copy(block).start()

        total = bx[y].astype(F32)
        for j in range(3):
            y0_copy(lax.rem(y + j + 1, NY)).wait_recv()
            total += ry[j].astype(F32)
        zown[...] = total

    @pl.when(core == 1)
    def _():
        total = chip[pl.ds(pl.multiple_of(half * y, 16), half), :].astype(F32)
        for j in range(3):
            y1_copy(lax.rem(y + j + 1, NY)).wait_recv()
            total += ry1[j].astype(F32)
        b1[...] = total.astype(BF16)
        for j in (1, 3, 2):
            x1_copy(j).start()
        total = b1[:, mine].astype(F32)
        for j in (1, 3, 2):
            x1_copy(j).wait_recv()
            total += rx1[j - 1].astype(F32)
        zown[...] = total

    for k in range(NZ):
        zp[k] = jnp.concatenate(
            [zown[56 * k : 56 * k + 56, :], jnp.zeros((8, LN), F32)], 0
        ).astype(BF16)

    def z_copy(j):
        zz = lax.rem(z + j, NZ)
        return remote(
            zp.at[zz], rz.at[j - 1], z_s.at[j - 1], z_r.at[j - 1], p + (zz - z) * NC, x
        )

    for j in range(1, NZ):
        z_copy(j).start()

    pltpu.make_async_copy(incb.at[pl.ds(0, DOM - 1)], incb.at[pl.ds(0, DOM - 1)], rb_r).wait()
    back = incb[...].astype(F32).reshape(4 * LN, LN).astype(BF16)
    slots = dot(back_o[...], back)
    stay_t = onehot(frow == iota((LN, ND), 0))
    latgrad_ref[...] = jnp.concatenate(
        [
            (
                dot(stay_t, node_grad[:, c * LN : (c + 1) * LN])
                + slots[c * ND : (c + 1) * ND, :]
            ).astype(BF16)
            for c in range(4)
        ],
        1,
    )

    total = zown[pl.ds(pl.multiple_of(56 * z, 8), 56), :]
    for j in range(1, NZ):
        z_copy(j).wait_recv()
        total += rz[j - 1].astype(F32)[:56, :]
    wgrad_ref[...] = total

    pltpu.make_async_copy(msg.at[pl.ds(0, DOM - 1)], msg.at[pl.ds(0, DOM - 1)], r_s).wait()
    pltpu.make_async_copy(msgb.at[pl.ds(0, DOM - 1)], msgb.at[pl.ds(0, DOM - 1)], rb_s).wait()
    for c in gathers + halos + scatters:
        c.wait_send()
    for block in range(4):
        core_copy(block).wait_send()

    @pl.when(core == 0)
    def _():
        for block in range(4):
            for j in (1, 3, 2):
                x_copy(block, j).wait_send()
        for j in range(3):
            y0_copy(lax.rem(y + j + 1, NY)).wait_send()

    @pl.when(core == 1)
    def _():
        for j in range(3):
            y1_copy(lax.rem(y + j + 1, NY)).wait_send()
        for j in (1, 3, 2):
            x1_copy(j).wait_send()

    for j in range(1, NZ):
        z_copy(j).wait_send()
    st_new.wait()
    st_grad.wait()


def body(
    tile_latent, relay_pick, relay_from, cut_pick, edge_latent, edge_sender, edge_receiver,
    edge_in, edge_out, node_in, node_out, node_cot, edge_cot,
):
    vmem = pl.BlockSpec(memory_space=pltpu.VMEM)
    hbm = pl.BlockSpec(memory_space=pl.ANY)
    dma = pltpu.SemaphoreType.DMA
    V = pltpu.VMEM
    half = 7 * ED // 12
    scratch = [
        V((ED, H), BF16), V((ED, H), BF16), V((3 * H, H), BF16), V((H, H), BF16),
        V((2 * H, H), BF16), V((H, H), BF16), dma((8,)),
        V((DOM, 8, LN), BF16), V((DOM, 8, LN), BF16), V((DOM, 8, LN), BF16), V((DOM, 8, LN), BF16),
        V((TR, H), BF16), V((ND, H), BF16), V((32, H), BF16),
        V((ED, TR), BF16), V((TR, ED), BF16), V((ED, 2 * LN), BF16), V((ND, ED), BF16),
        V((4 * ND, 4 * LN), BF16), V((4 * ND, 4 * LN), BF16), V((4 * LN, 4 * ND), BF16),
        V((ED, H), F32), V((ED, H), BF16), V((ED, H), F32), V((ED, H), F32), V((ED, LN), F32),
        V((ED, H), BF16), V((ED, H), BF16), V((ED, H), BF16), V((ED, H), BF16),
        V((TR, H), F32), V((TR, H), BF16), V((3, ND, H), BF16), V((32, H), BF16), V((7 * H, H), F32),
        V((4 * half, H), BF16), V((4 * half, H), BF16), V((4 * half, H), BF16),
        V((12, half, LN), BF16), V((4, half, LN), BF16), V((3, half, LN), BF16),
        V((3, half, H), BF16), V((half, H), BF16), V((3, half, LN), BF16),
        V((half, LN), F32), V((NZ, 64, LN), BF16), V((NZ - 1, 64, LN), BF16),
        dma, dma, dma((5,)), dma((5,)), dma, dma, dma((5,)), dma((5,)), dma((4,)), dma((4,)),
        dma((12,)), dma((12,)), dma((3,)), dma((3,)), dma((NZ - 1,)), dma((NZ - 1,)),
    ]
    return pl.pallas_call(
        kernel,
        out_shape=(
            jax.ShapeDtypeStruct((ND, H), BF16),
            jax.ShapeDtypeStruct((ED, H), BF16),
            jax.ShapeDtypeStruct((ND, H), BF16),
            jax.ShapeDtypeStruct((ED, H), BF16),
            jax.ShapeDtypeStruct((56, LN), F32),
        ),
        in_specs=[vmem] * 7 + [hbm] * 6,
        out_specs=(vmem, hbm, vmem, hbm, vmem),
        scratch_shapes=scratch,
        compiler_params=pltpu.CompilerParams(
            collective_id=0, has_side_effects=True, vmem_limit_bytes=56 * 2**20
        ),
    )(
        tile_latent, relay_pick, relay_from.reshape(1, ND), cut_pick,
        edge_sender.reshape(ED // LN, LN), edge_receiver.reshape(ED // LN, LN), node_cot,
        edge_latent, edge_cot, edge_in, edge_out, node_in, node_out,
    )


def solution(mesh):
    rows = P(("dom", "tile"), None)
    flat = P(("dom", "tile"))
    in_specs = (
        rows, rows, flat, rows, rows, flat, flat, P(), P(), P(), P(), rows, rows,
    )
    out_specs = (rows, rows, rows, rows, P("dom", "tile"))
    return jax.shard_map(body, mesh=mesh, in_specs=in_specs, out_specs=out_specs, check_vma=False)
```

time: 294 us -> 80 us (0.27)
  waiting for transfers between devices: 160 us -> 0 us
  Pallas kernels: 0 us -> 73.3 us
  matrix products: 35.4 us -> 0 us
  local copies, waits for them, and re-layouts: 32.2 us -> 5.87 us
  starting transfers between devices: 26.2 us -> 0 us
  between operations: 14.6 us -> 0.66 us
  other arithmetic: 11.7 us -> 0 us
  blocking collectives: 11.4 us -> 0 us
    reduce_scatter x3 -> x0, waiting for transfers between devices: 155 us -> none  [the longest x1 134 us: body(): lax.psum_scatter(weight_terms, 'dom', scatter_dimension=0, tiled=True)]
    pallas_call x0 -> x1, Pallas kernels: none -> 73.3 us  [body(): pl.pallas_call(kernel, out_shape=(jax.ShapeDtypeStruct((ND, H), BF16), ja...]
    dot_general x26 -> x0, matrix products: 35.4 us -> none  [the longest x12 17.1 us: inner_dot(): lax.dot_general(left_mat, right_mat, (((0,), (0,)), ((), ())), preferred_...]
    all_to_all x2 -> x0, starting transfers between devices: 21.9 us -> none  [the longest x1 13.2 us: body(): lax.all_to_all(outgoing, 'dom', split_axis=0, concat_axis=0, tiled=True)]
    gather x9 -> x0, local copies, waits for them, and re-layouts: 17.4 us -> none  [the longest x2 4.97 us: body(): jnp.take(agg_grad, edge_receiver, axis=0)]
    all_gather x1 -> x0, blocking collectives: 11.4 us -> none  [body(): part_rows = lax.all_gather(latent, 'tile', axis=0, tiled=True)]
    all_to_all x2 -> x0, waiting for transfers between devices: 5.79 us -> none  [the longest x1 5.79 us: body(): lax.all_to_all(outgoing, 'dom', split_axis=0, concat_axis=0, tiled=True)]
    unnamed x101 -> x11, local copies, waits for them, and re-layouts: 11.3 us -> 5.87 us
  transfers between devices with their start and end apart: 9 -> 0, of which waited for: 3 -> 0; matrix products, arithmetic and copies ran while one was open for 14% -> 0% of each run, Pallas kernels for 0% -> 0%
where the time goes in v1:
time: 80 us; the launch traced here: 79.8 us
  Pallas kernels  73.3 us (92%)
  local copies, waits for them, and re-layouts  5.87 us (7%)
    pallas_call x1, Pallas kernels, body(): pl.pallas_call(kernel, out_shape=(jax.ShapeDtypeStruct((ND, H), BF16), ja...  73.3 us
    unnamed x11, local copies, waits for them, and re-layouts  5.87 us

profile of v1, /device:TPU:1, one launch (start us, length us, event | category | flops | bytes accessed | tf_op | source)
XLA Modules:
  0.0 79.8 jit_solution(15798104187370090767)
XLA Ops:
  0.6 73.3 %shard_map.164 = (bf16[128,512]{1,0:T(8,128)(2,1)}, bf16[768,512]{1,0:T(8,128)(2,1)}, bf16[128,512]{1,0:T(8,128)(2,1)}, bf16[768,512]{1,0:T(8,128)(2,1)}, f32[56,128]{1,0:T(8,128)}) custom-call(bf16[128,512]{1,0:T(8,128)(2,1)} %tile_ref.1, s32[1,128]{1,0:T(1,128)} %pick_ref.1, s32[1,128]{1,0:T(1,128)} %bitcast.5, s32[1,32]{1,0:T(1,128)} %cut_ref.1, ...), custom_call_target="tpu_custom_call" | custom-call | tf_op jit(solution)/shard_map/pallas_call | solution.py:533
  73.9 0.0 copy-start.1
  73.9 0.0 copy-start
  73.9 1.6 %copy.23 = bf16[128,512]{1,0:T(8,128)(2,1)} copy(bf16[128,512]{1,0:T(8,128)(2,1)} %get-tuple-element.10) | data formatting | bytes 262144
  75.6 0.0 copy-start.2
  75.6 2.1 %copy.24 = bf16[768,512]{1,0:T(8,128)(2,1)} copy(bf16[768,512]{1,0:T(8,128)(2,1)} %get-tuple-element.11) | data formatting | bytes 1572864
  77.7 0.0 copy-done.1
  77.7 0.7 copy.25
  78.3 0.0 copy-done
  78.3 0.9 %copy.26 = bf16[768,512]{1,0:T(8,128)(2,1)} copy(bf16[768,512]{1,0:T(8,128)(2,1)S(1)} %copy-done) | data formatting | bytes 1572864
  79.2 0.0 copy-done.2
  79.2 0.6 copy.27
Async XLA Ops:
  73.9 3.7 %copy-start.1 = (bf16[128,512]{1,0:T(8,128)(2,1)S(1)}, bf16[128,512]{1,0:T(8,128)(2,1)}, u32[]{:S(2)}) copy-start(bf16[128,512]{1,0:T(8,128)(2,1)} %get-tuple-element.12) | copy-start | bytes 393220
  73.9 4.4 %copy-start = (bf16[768,512]{1,0:T(8,128)(2,1)S(1)}, bf16[768,512]{1,0:T(8,128)(2,1)}, u32[]{:S(2)}) copy-start(bf16[768,512]{1,0:T(8,128)(2,1)} %get-tuple-element.13) | copy-start | bytes 2359300
  75.6 3.6 %copy-start.2 = (f32[56,128]{1,0:T(8,128)S(1)}, f32[56,128]{1,0:T(8,128)}, u32[]{:S(2)}) copy-start(f32[56,128]{1,0:T(8,128)} %get-tuple-element.14) | copy-start | bytes 86020

commit v2 on v1

--- a/solution.py
+++ b/solution.py
@@ -17,6 +17,9 @@
 EB = 256
 TR = 640
 LN = 128
+SUB = 224
+RX = 112
+RY = SUB - RX
 
 
 def iota(shape, dim):
@@ -71,8 +74,9 @@
     sel_s, sel_st, sel_r, sel_rt, gat_i, back_o, back_p,
     pre, act, dsilu, normed, einv, enew, egrad, plg, ppg,
     gsum, gs, gr, hb, wg,
-    csend, crecv, chip, rx, bx, ry, ry1, b1, rx1, zown, zp, rz,
-    r_s, r_r, a_s, a_r, rb_s, rb_r, g_s, g_r, c_s, c_r, s2_s, s2_r, s3_s, s3_r, z_s, z_r,
+    csend, crecv, chip, rx, bx, ry, ry1, b1, rx2, zown, zp, rz,
+    r_s, r_r, a_s, a_r, rb_s, rb_r, g_s, g_r, c_s, c_r,
+    x1_s, x1_r, y1_s, y1_r, y2_s, y2_r, x2_s, x2_r, z_s, z_r,
 ):
     p = lax.axis_index("dom")
     x = lax.axis_index("tile")
@@ -269,10 +273,8 @@
     wg[5 * H : 6 * H, :] = dot_tn(agg, npg)
     wg[6 * H :, :] = dot_tn(node_act, nlg)
 
-    half = 7 * ED // 12
-
     def two_blocks(block, k, side):
-        base = 2 * half * block + 4 * 56 * k + 56 * side
+        base = 2 * SUB * block + 4 * 56 * k + 56 * side
         return jnp.concatenate(
             [
                 wg[pl.ds(pl.multiple_of(base, 8), 56), :],
@@ -282,68 +284,87 @@
         )
 
     def core_copy(block):
-        rows = pl.ds(half * block, half)
+        rows = pl.ds(SUB * block, SUB)
         return remote(
             csend.at[rows], crecv.at[rows], c_s.at[block], c_r.at[block], sib, x
         )
 
     def pack_core(block):
-        def body(k, carry):
-            rows = pl.ds(pl.multiple_of(half * block + 112 * k, 16), 112)
+        for k in range(2):
+            rows = pl.ds(SUB * block + 112 * k, 112)
             csend[rows, :] = two_blocks(block, k, 1 - core).astype(BF16)
-            return carry
-
-        lax.fori_loop(0, 4, body, 0)
         core_copy(block).start()
 
-    def x_copy(block, j):
+    def columns(t):
+        return pl.ds(pl.multiple_of(t * LN, LN), LN)
+
+    def x1_copy(block, j):
         t = xpeer(j)
-        cols = pl.ds(pl.multiple_of(t * LN, LN), LN)
         i = 3 * block + j - 1
         return remote(
-            chip.at[pl.ds(half * block, half), cols], rx.at[i], s2_s.at[i], s2_r.at[i], p, t
-        )
-
-    def y_index(block):
-        return lax.rem(block - y + NY, NY)
+            chip.at[pl.ds(SUB * block, RX), columns(t)], rx.at[i], x1_s.at[i], x1_r.at[i], p, t
+        )
 
     def y_copy(src, dst, ss, rs, block):
-        j = y_index(block) - 1
-        return remote(src, dst.at[j], ss.at[j], rs.at[j], p + (block - y) * NC * NZ, x)
+        i = 2 * (lax.rem(block // 2 - y + NY, NY) - 1) + block % 2
+        return remote(
+            src, dst.at[i], ss.at[i], rs.at[i], p + (block // 2 - y) * NC * NZ, x
+        )
 
     def y1_copy(block):
-        return y_copy(chip.at[pl.ds(half * block, half)], ry1, s3_s, s3_r, block)
-
-    def y0_copy(block):
-        return y_copy(bx.at[block], ry, s3_s, s3_r, block)
-
-    def x1_copy(j):
+        return y_copy(chip.at[pl.ds(SUB * block + RX, RY)], ry1, y1_s, y1_r, block)
+
+    def y2_copy(block):
+        return y_copy(bx.at[block], ry, y2_s, y2_r, block)
+
+    def x2_copy(s, j):
         t = xpeer(j)
-        cols = pl.ds(pl.multiple_of(t * LN, LN), LN)
-        return remote(b1.at[:, cols], rx1.at[j - 1], s2_s.at[j - 1], s2_r.at[j - 1], p, t)
+        i = 3 * s + j - 1
+        return remote(b1.at[s, :, columns(t)], rx2.at[i], x2_s.at[i], x2_r.at[i], p, t)
+
+    def y_block(j, s):
+        return 2 * lax.rem(y + j, NY) + s
 
     def combine(block):
         core_copy(block).wait_recv()
-
-        def body(k, carry):
-            rows = pl.ds(pl.multiple_of(half * block + 112 * k, 16), 112)
+        for k in range(2):
+            rows = pl.ds(SUB * block + 112 * k, 112)
             chip[rows, :] = (
                 two_blocks(block, k, core) + crecv[rows, :].astype(F32)
             ).astype(BF16)
-            return carry
-
-        lax.fori_loop(0, 4, body, 0)
-
-        @pl.when(core == 0)
-        def _():
-            for j in (1, 3, 2):
-                x_copy(block, j).start()
-
-        @pl.when((core == 1) & (y != block))
+
+        @pl.when(y != block // 2)
         def _():
             y1_copy(block).start()
 
-    pack_core(3)
+        for j in (1, 3, 2):
+            x1_copy(block, j).start()
+
+    mine = columns(x)
+
+    def finish_x(block):
+        total = chip[pl.ds(SUB * block, RX), mine].astype(F32)
+        for j in (1, 3, 2):
+            x1_copy(block, j).wait_recv()
+            total += rx[3 * block + j - 1].astype(F32)
+        bx[block] = total.astype(BF16)
+
+        @pl.when(y != block // 2)
+        def _():
+            y2_copy(block).start()
+
+    def finish_y(s):
+        own = pl.ds(pl.multiple_of(SUB * (2 * y + s) + RX, 16), RY)
+        total = chip[own, :].astype(F32)
+        for j in range(1, NY):
+            y1_copy(y_block(j, s)).wait_recv()
+            total += ry1[2 * (j - 1) + s].astype(F32)
+        b1[s] = total.astype(BF16)
+        for j in (1, 3, 2):
+            x2_copy(s, j).start()
+
+    for block in (7, 6, 5):
+        pack_core(block)
 
     def edge_backward(b, carry):
         rows = pl.ds(pl.multiple_of(b * EB, EB), EB)
@@ -355,7 +376,10 @@
         egrad[rows, :] = (upst + dot_nt(pg, ein[:H, :])).astype(BF16)
         return carry
 
-    lax.fori_loop(0, ED // EB, edge_backward, 0)
+    lax.fori_loop(0, 1, edge_backward, 0)
+    for block in (7, 6, 5):
+        combine(block)
+    lax.fori_loop(1, ED // EB, edge_backward, 0)
     gsum[...] = dot(sel_st[...], ppg[...])
     gs[...] = gsum[...].astype(BF16)
 
@@ -373,18 +397,19 @@
         c.start()
     st_grad = pltpu.make_async_copy(egrad, edgegrad_hbm, lsem.at[7])
     st_grad.start()
-    combine(3)
     wg[3 * H : 4 * H, :] = dot_tn(act[...], plg[...])
-    pack_core(2)
     grecv = dot(sel_rt[...], ppg[...]).astype(BF16)
+    wg[2 * H : 3 * H, :] = dot_tn(latent, grecv)
+    pack_core(3)
+    wg[H : 2 * H, :] = dot_tn(table[...], gs[...])
+    wg[:H, :] = dot_tn(e[...], ppg[...])
+    for block in (1, 2, 0, 4):
+        pack_core(block)
     node_part = node_direct + dot_nt(grecv, ein[2 * H :, :])
-    wg[2 * H : 3 * H, :] = dot_tn(latent, grecv)
-    wg[H : 2 * H, :] = dot_tn(table[...], gs[...])
-    pack_core(1)
-    combine(2)
-    wg[:H, :] = dot_tn(e[...], ppg[...])
-    pack_core(0)
-    combine(1)
+    for block in (3, 1, 2, 0, 4):
+        combine(block)
+    for block in (7, 6, 5):
+        finish_x(block)
 
     for c in scatters:
         c.wait_recv()
@@ -403,57 +428,41 @@
         return carry
 
     lax.fori_loop(1, DOM, relay_back, 0)
-    combine(0)
-
-    mine = pl.ds(pl.multiple_of(x * LN, LN), LN)
-
-    @pl.when(core == 0)
-    def _():
-        for block in (3, 2, 1, 0):
-            total = chip[pl.ds(half * block, half), mine].astype(F32)
-            for j in (1, 3, 2):
-                x_copy(block, j).wait_recv()
-                total += rx[3 * block + j - 1].astype(F32)
-            bx[block] = total.astype(BF16)
-
-            @pl.when(y != block)
+
+    def z_copy(t):
+        i = lax.rem(t - z + NZ, NZ) - 1
+        return remote(zp.at[t], rz.at[i], z_s.at[i], z_r.at[i], p + (t - z) * NC, x)
+
+    def half_sum(s):
+        part = bx[2 * y + s].astype(F32)
+        for j in range(1, NY):
+            y2_copy(y_block(j, s)).wait_recv()
+            part += ry[2 * (j - 1) + s].astype(F32)
+        rest = b1[s, :, mine].astype(F32)
+        for j in (1, 3, 2):
+            x2_copy(s, j).wait_recv()
+            rest += rx2[3 * s + j - 1].astype(F32)
+        total = jnp.concatenate([part, rest], 0)
+        zown[SUB * s : SUB * (s + 1), :] = total
+        for k in range(4):
+            zp[4 * s + k] = jnp.concatenate(
+                [total[56 * k : 56 * k + 56, :], jnp.zeros((8, LN), F32)], 0
+            ).astype(BF16)
+        for k in range(4):
+            t = 4 * s + k
+
+            @pl.when(t != z)
             def _():
-                y0_copy(block).start()
-
-        total = bx[y].astype(F32)
-        for j in range(3):
-            y0_copy(lax.rem(y + j + 1, NY)).wait_recv()
-            total += ry[j].astype(F32)
-        zown[...] = total
-
-    @pl.when(core == 1)
-    def _():
-        total = chip[pl.ds(pl.multiple_of(half * y, 16), half), :].astype(F32)
-        for j in range(3):
-            y1_copy(lax.rem(y + j + 1, NY)).wait_recv()
-            total += ry1[j].astype(F32)
-        b1[...] = total.astype(BF16)
-        for j in (1, 3, 2):
-            x1_copy(j).start()
-        total = b1[:, mine].astype(F32)
-        for j in (1, 3, 2):
-            x1_copy(j).wait_recv()
-            total += rx1[j - 1].astype(F32)
-        zown[...] = total
-
-    for k in range(NZ):
-        zp[k] = jnp.concatenate(
-            [zown[56 * k : 56 * k + 56, :], jnp.zeros((8, LN), F32)], 0
-        ).astype(BF16)
-
-    def z_copy(j):
-        zz = lax.rem(z + j, NZ)
-        return remote(
-            zp.at[zz], rz.at[j - 1], z_s.at[j - 1], z_r.at[j - 1], p + (zz - z) * NC, x
-        )
-
-    for j in range(1, NZ):
-        z_copy(j).start()
+                z_copy(t).start()
+
+    for block in (3, 1):
+        finish_x(block)
+    finish_y(1)
+    for block in (4, 2, 0):
+        finish_x(block)
+    finish_y(0)
+    half_sum(1)
+    half_sum(0)
 
     pltpu.make_async_copy(incb.at[pl.ds(0, DOM - 1)], incb.at[pl.ds(0, DOM - 1)], rb_r).wait()
     back = incb[...].astype(F32).reshape(4 * LN, LN).astype(BF16)
@@ -472,7 +481,7 @@
 
     total = zown[pl.ds(pl.multiple_of(56 * z, 8), 56), :]
     for j in range(1, NZ):
-        z_copy(j).wait_recv()
+        z_copy(lax.rem(z + j, NZ)).wait_recv()
         total += rz[j - 1].astype(F32)[:56, :]
     wgrad_ref[...] = total
 
@@ -480,28 +489,24 @@
     pltpu.make_async_copy(msgb.at[pl.ds(0, DOM - 1)], msgb.at[pl.ds(0, DOM - 1)], rb_s).wait()
     for c in gathers + halos + scatters:
         c.wait_send()
-    for block in range(4):
+    for block in range(8):
         core_copy(block).wait_send()
-
-    @pl.when(core == 0)
-    def _():
-        for block in range(4):
-            for j in (1, 3, 2):
-                x_copy(block, j).wait_send()
-        for j in range(3):
-            y0_copy(lax.rem(y + j + 1, NY)).wait_send()
-
-    @pl.when(core == 1)
-    def _():
-        for j in range(3):
-            y1_copy(lax.rem(y + j + 1, NY)).wait_send()
         for j in (1, 3, 2):
-            x1_copy(j).wait_send()
-
+            x1_copy(block, j).wait_send()
+    for s in range(2):
+        for j in range(1, NY):
+            y1_copy(y_block(j, s)).wait_send()
+            y2_copy(y_block(j, s)).wait_send()
+            x2_copy(s, j).wait_send()
     for j in range(1, NZ):
-        z_copy(j).wait_send()
+        z_copy(lax.rem(z + j, NZ)).wait_send()
     st_new.wait()
     st_grad.wait()
+
+
+def hand_over(*refs):
+    for a, b in zip(refs[:5], refs[5:]):
+        b[...] = a[...]
 
 
 def body(
@@ -512,7 +517,6 @@
     hbm = pl.BlockSpec(memory_space=pl.ANY)
     dma = pltpu.SemaphoreType.DMA
     V = pltpu.VMEM
-    half = 7 * ED // 12
     scratch = [
         V((ED, H), BF16), V((ED, H), BF16), V((3 * H, H), BF16), V((H, H), BF16),
         V((2 * H, H), BF16), V((H, H), BF16), dma((8,)),
@@ -523,22 +527,24 @@
         V((ED, H), F32), V((ED, H), BF16), V((ED, H), F32), V((ED, H), F32), V((ED, LN), F32),
         V((ED, H), BF16), V((ED, H), BF16), V((ED, H), BF16), V((ED, H), BF16),
         V((TR, H), F32), V((TR, H), BF16), V((3, ND, H), BF16), V((32, H), BF16), V((7 * H, H), F32),
-        V((4 * half, H), BF16), V((4 * half, H), BF16), V((4 * half, H), BF16),
-        V((12, half, LN), BF16), V((4, half, LN), BF16), V((3, half, LN), BF16),
-        V((3, half, H), BF16), V((half, H), BF16), V((3, half, LN), BF16),
-        V((half, LN), F32), V((NZ, 64, LN), BF16), V((NZ - 1, 64, LN), BF16),
-        dma, dma, dma((5,)), dma((5,)), dma, dma, dma((5,)), dma((5,)), dma((4,)), dma((4,)),
-        dma((12,)), dma((12,)), dma((3,)), dma((3,)), dma((NZ - 1,)), dma((NZ - 1,)),
+        V((8 * SUB, H), BF16), V((8 * SUB, H), BF16), V((8 * SUB, H), BF16),
+        V((24, RX, LN), BF16), V((8, RX, LN), BF16), V((6, RX, LN), BF16),
+        V((6, RY, H), BF16), V((2, RY, H), BF16), V((6, RY, LN), BF16),
+        V((2 * SUB, LN), F32), V((NZ, 64, LN), BF16), V((NZ - 1, 64, LN), BF16),
+        dma, dma, dma((5,)), dma((5,)), dma, dma, dma((5,)), dma((5,)), dma((8,)), dma((8,)),
+        dma((24,)), dma((24,)), dma((6,)), dma((6,)), dma((6,)), dma((6,)), dma((6,)), dma((6,)),
+        dma((NZ - 1,)), dma((NZ - 1,)),
     ]
-    return pl.pallas_call(
+    shapes = (
+        jax.ShapeDtypeStruct((ND, H), BF16),
+        jax.ShapeDtypeStruct((ED, H), BF16),
+        jax.ShapeDtypeStruct((ND, H), BF16),
+        jax.ShapeDtypeStruct((ED, H), BF16),
+        jax.ShapeDtypeStruct((56, LN), F32),
+    )
+    parts = pl.pallas_call(
         kernel,
-        out_shape=(
-            jax.ShapeDtypeStruct((ND, H), BF16),
-            jax.ShapeDtypeStruct((ED, H), BF16),
-            jax.ShapeDtypeStruct((ND, H), BF16),
-            jax.ShapeDtypeStruct((ED, H), BF16),
-            jax.ShapeDtypeStruct((56, LN), F32),
-        ),
+        out_shape=shapes,
         in_specs=[vmem] * 7 + [hbm] * 6,
         out_specs=(vmem, hbm, vmem, hbm, vmem),
         scratch_shapes=scratch,
@@ -550,6 +556,13 @@
         edge_sender.reshape(ED // LN, LN), edge_receiver.reshape(ED // LN, LN), node_cot,
         edge_latent, edge_cot, edge_in, edge_out, node_in, node_out,
     )
+    return pl.pallas_call(
+        hand_over,
+        out_shape=shapes,
+        in_specs=[vmem] * 5,
+        out_specs=(vmem,) * 5,
+        compiler_params=pltpu.CompilerParams(vmem_limit_bytes=60 * 2**20),
+    )(*parts)
 
 
 def solution(mesh):

time: 80 us -> 68.5 us (0.86)
  local copies, waits for them, and re-layouts: 5.87 us -> 0 us
  Pallas kernels: 73.3 us -> 67.7 us
    unnamed x11 -> x0, local copies, waits for them, and re-layouts: 5.87 us -> none
    pallas_call x1 -> x2, Pallas kernels: 73.3 us -> 67.7 us  [the longest x1 65 us: body(): pl.pallas_call(kernel, out_shape=shapes, in_specs=[vmem] * 7 + [hbm] * 6,...]
where the time goes in v2:
time: 68.5 us; the launch traced here: 68.4 us
  Pallas kernels  67.7 us (99%)
    pallas_call x1, Pallas kernels, body(): pl.pallas_call(kernel, out_shape=shapes, in_specs=[vmem] * 7 + [hbm] * 6,...  65 us
    pallas_call x1, Pallas kernels, body(): pl.pallas_call(hand_over, out_shape=shapes, in_specs=[vmem] * 5, out_spec...  2.69 us

profile of v2, /device:TPU:1, one launch (start us, length us, event | category | flops | bytes accessed | tf_op | source)
XLA Modules:
  0.0 68.4 jit_solution(17020348536687241445)
XLA Ops:
  0.6 65.0 %shard_map.164 = (bf16[128,512]{1,0:T(8,128)(2,1)}, bf16[768,512]{1,0:T(8,128)(2,1)}, bf16[128,512]{1,0:T(8,128)(2,1)}, bf16[768,512]{1,0:T(8,128)(2,1)}, f32[56,128]{1,0:T(8,128)}) custom-call(bf16[128,512]{1,0:T(8,128)(2,1)} %tile_ref.1, s32[1,128]{1,0:T(1,128)} %pick_ref.1, s32[1,128]{1,0:T(1,128)} %bitcast.5, s32[1,32]{1,0:T(1,128)} %cut_ref.1, ...), custom_call_target="tpu_custom_call" | custom-call | tf_op jit(solution)/shard_map/pallas_call | solution.py:545
  65.7 2.7 %shard_map.165 = (bf16[128,512]{1,0:T(8,128)(2,1)}, bf16[768,512]{1,0:T(8,128)(2,1)}, bf16[128,512]{1,0:T(8,128)(2,1)}, bf16[768,512]{1,0:T(8,128)(2,1)}, f32[56,128]{1,0:T(8,128)}) custom-call(bf16[128,512]{1,0:T(8,128)(2,1)} %get-tuple-element.10.refs_0_, bf16[768,512]{1,0:T(8,128)(2,1)} %get-tuple-element.11.refs_1_, ...), custom_call_target="tpu_custom_call" | custom-call | tf_op jit(solution)/shard_map/pallas_call | solution.py:559

commit v3 on v2

--- a/solution.py
+++ b/solution.py
@@ -14,7 +14,8 @@
 H = 512
 ND = 128
 ED = 768
-EB = 256
+EB = 384
+EF = 768
 TR = 640
 LN = 128
 SUB = 224
@@ -68,11 +69,11 @@
 def kernel(
     tile_ref, pick_ref, from_ref, cut_ref, snd_ref, rcv_ref, ncot_ref,
     e_hbm, cot_hbm, ein_hbm, eout_hbm, nin_hbm, nout_hbm,
-    nodeup_ref, edgeup_hbm, latgrad_ref, edgegrad_hbm, wgrad_ref,
+    nodeup_ref, enew, latgrad_ref, egrad, wgrad_ref,
     e, cot, ein, eout, nin, nout, lsem,
     msg, inc, msgb, incb, table, lat, halo_s,
     sel_s, sel_st, sel_r, sel_rt, gat_i, back_o, back_p,
-    pre, act, dsilu, normed, einv, enew, egrad, plg, ppg,
+    pre, act, dsilu, normed, einv, plg, ppg,
     gsum, gs, gr, hb, wg,
     csend, crecv, chip, rx, bx, ry, ry1, b1, rx2, zown, zp, rz,
     r_s, r_r, a_s, a_r, rb_s, rb_r, g_s, g_r, c_s, c_r,
@@ -135,12 +136,24 @@
 
     pl.semaphore_wait(barrier, DOM - 1 + NX - 1)
 
-    def relay(i, carry):
-        q = lax.rem(p + i, DOM)
-        remote(msg.at[q], inc.at[p], r_s, r_r, q, x).start()
-        return carry
-
-    lax.fori_loop(1, DOM, relay, 0)
+    def exchange(src, dst, ss, rs):
+        def step(i, last):
+            dz = NZ // 2 + (i + 1) // 2 * (1 - 2 * (i % 2))
+            for dy in (2, 1, 3, 0):
+                for dc in (0, 1):
+                    if not last or dy or dc:
+                        q = lax.rem(y + dy, NY) * (NZ * NC)
+                        q += lax.rem(z + dz, NZ) * NC + lax.rem(core + dc, NC)
+                        remote(src.at[q], dst.at[p], ss, rs, q, x).start()
+
+        def loop(i, carry):
+            step(i, False)
+            return carry
+
+        lax.fori_loop(0, NZ - 1, loop, 0)
+        step(NZ - 1, True)
+
+    exchange(msg, inc, r_s, r_r)
 
     frow = jnp.broadcast_to(from_ref[...], (LN, ND))
     fcol = frow.T
@@ -176,11 +189,11 @@
     loads[1].wait()
 
     def edge_term(b, carry):
-        rows = pl.ds(pl.multiple_of(b * EB, EB), EB)
+        rows = pl.ds(pl.multiple_of(b * EF, EF), EF)
         pre[rows, :] = dot(e[rows, :], ein[:H, :])
         return carry
 
-    lax.fori_loop(0, ED // EB, edge_term, 0)
+    lax.fori_loop(0, ED // EF, edge_term, 0)
 
     pltpu.make_async_copy(inc.at[pl.ds(0, DOM - 1)], inc.at[pl.ds(0, DOM - 1)], r_r).wait()
     got = inc[...].astype(F32).reshape(4 * LN, LN).astype(BF16)
@@ -220,11 +233,11 @@
     recv_proj = jnp.concatenate([rh, rl], 0)
 
     def recv_term(b, carry):
-        rows = pl.ds(pl.multiple_of(b * EB, EB), EB)
+        rows = pl.ds(pl.multiple_of(b * EF, EF), EF)
         pre[rows, :] += dot(sel_r[rows, :], recv_proj)
         return carry
 
-    lax.fori_loop(0, ED // EB, recv_term, 0)
+    lax.fori_loop(0, ED // EF, recv_term, 0)
     prow = dot_nt(pickb, quad)
     pq = iota((ND, 4 * LN), 1) % 4
     pn = iota((ND, 4 * LN), 0).astype(F32)
@@ -242,7 +255,7 @@
         c.wait_recv()
 
     def edge_forward(b, carry):
-        rows = pl.ds(pl.multiple_of(b * EB, EB), EB)
+        rows = pl.ds(pl.multiple_of(b * EF, EF), EF)
         send_rows = dot(sel_s[rows, :], table[...]).astype(BF16)
         a, da = silu_pair(pre[rows, :] + dot(send_rows, ein[H : 2 * H, :]))
         a = a.astype(BF16)
@@ -250,13 +263,11 @@
         dsilu[rows, :] = da
         yn, inv = norm(dot(a, eout[...]))
         normed[rows, :] = yn
-        einv[rows, :] = jnp.broadcast_to(inv, (EB, LN))
+        einv[rows, :] = jnp.broadcast_to(inv, (EF, LN))
         enew[rows, :] = (e[rows, :].astype(F32) + yn).astype(BF16)
         return carry
 
-    lax.fori_loop(0, ED // EB, edge_forward, 0)
-    st_new = pltpu.make_async_copy(enew, edgeup_hbm, lsem.at[6])
-    st_new.start()
+    lax.fori_loop(0, ED // EF, edge_forward, 0)
 
     agg = dot(sel_rt[...], enew[...]).astype(BF16)
     node_act, node_dsilu = silu_pair(dot(latent, nin[:H, :]) + dot(agg, nin[H:, :]))
@@ -395,8 +406,6 @@
     ]
     for c in scatters:
         c.start()
-    st_grad = pltpu.make_async_copy(egrad, edgegrad_hbm, lsem.at[7])
-    st_grad.start()
     wg[3 * H : 4 * H, :] = dot_tn(act[...], plg[...])
     grecv = dot(sel_rt[...], ppg[...]).astype(BF16)
     wg[2 * H : 3 * H, :] = dot_tn(latent, grecv)
@@ -422,12 +431,7 @@
     ng = jnp.concatenate([node_grad[:, c * LN : (c + 1) * LN] for c in range(4)], 0)
     msgb[...] = dot(back_p[...], ng).reshape(DOM, 8, LN).astype(BF16)
 
-    def relay_back(i, carry):
-        q = lax.rem(p + i, DOM)
-        remote(msgb.at[q], incb.at[p], rb_s, rb_r, q, x).start()
-        return carry
-
-    lax.fori_loop(1, DOM, relay_back, 0)
+    exchange(msgb, incb, rb_s, rb_r)
 
     def z_copy(t):
         i = lax.rem(t - z + NZ, NZ) - 1
@@ -500,13 +504,18 @@
             x2_copy(s, j).wait_send()
     for j in range(1, NZ):
         z_copy(lax.rem(z + j, NZ)).wait_send()
-    st_new.wait()
-    st_grad.wait()
 
 
 def hand_over(*refs):
-    for a, b in zip(refs[:5], refs[5:]):
-        b[...] = a[...]
+    sem = refs[-1]
+    copies = [
+        pltpu.make_async_copy(a, b, sem.at[i])
+        for i, (a, b) in enumerate(zip(refs[:5], refs[5:10]))
+    ]
+    for c in copies:
+        c.start()
+    for c in copies:
+        c.wait()
 
 
 def body(
@@ -525,7 +534,7 @@
         V((ED, TR), BF16), V((TR, ED), BF16), V((ED, 2 * LN), BF16), V((ND, ED), BF16),
         V((4 * ND, 4 * LN), BF16), V((4 * ND, 4 * LN), BF16), V((4 * LN, 4 * ND), BF16),
         V((ED, H), F32), V((ED, H), BF16), V((ED, H), F32), V((ED, H), F32), V((ED, LN), F32),
-        V((ED, H), BF16), V((ED, H), BF16), V((ED, H), BF16), V((ED, H), BF16),
+        V((ED, H), BF16), V((ED, H), BF16),
         V((TR, H), F32), V((TR, H), BF16), V((3, ND, H), BF16), V((32, H), BF16), V((7 * H, H), F32),
         V((8 * SUB, H), BF16), V((8 * SUB, H), BF16), V((8 * SUB, H), BF16),
         V((24, RX, LN), BF16), V((8, RX, LN), BF16), V((6, RX, LN), BF16),
@@ -535,6 +544,12 @@
         dma((24,)), dma((24,)), dma((6,)), dma((6,)), dma((6,)), dma((6,)), dma((6,)), dma((6,)),
         dma((NZ - 1,)), dma((NZ - 1,)),
     ]
+    held = tuple(
+        pltpu.VMEM(s, d)
+        for s, d in (
+            ((ND, H), BF16), ((ED, H), BF16), ((ND, H), BF16), ((ED, H), BF16), ((56, LN), F32),
+        )
+    )
     shapes = (
         jax.ShapeDtypeStruct((ND, H), BF16),
         jax.ShapeDtypeStruct((ED, H), BF16),
@@ -544,9 +559,9 @@
     )
     parts = pl.pallas_call(
         kernel,
-        out_shape=shapes,
+        out_shape=held,
         in_specs=[vmem] * 7 + [hbm] * 6,
-        out_specs=(vmem, hbm, vmem, hbm, vmem),
+        out_specs=(vmem,) * 5,
         scratch_shapes=scratch,
         compiler_params=pltpu.CompilerParams(
             collective_id=0, has_side_effects=True, vmem_limit_bytes=56 * 2**20
@@ -560,8 +575,9 @@
         hand_over,
         out_shape=shapes,
         in_specs=[vmem] * 5,
-        out_specs=(vmem,) * 5,
-        compiler_params=pltpu.CompilerParams(vmem_limit_bytes=60 * 2**20),
+        out_specs=(hbm,) * 5,
+        scratch_shapes=[dma((5,))],
+        compiler_params=pltpu.CompilerParams(vmem_limit_bytes=2**20),
     )(*parts)
 
 

time: 68.5 us -> 63.4 us (0.926)
  Pallas kernels: 67.7 us -> 62.4 us
    pallas_call x1, Pallas kernels: 65 us -> 61.1 us  [body(): pl.pallas_call(kernel, out_shape=held, in_specs=[vmem] * 7 + [hbm] * 6, o...]
    pallas_call x1, Pallas kernels: 2.69 us -> 1.27 us  [body(): pl.pallas_call(hand_over, out_shape=shapes, in_specs=[vmem] * 5, out_spec...]
where the time goes in v3:
time: 63.4 us; the launch traced here: 63 us
  Pallas kernels  62.4 us (98%)
  between operations  0.64 us (1%)
    pallas_call x1, Pallas kernels, body(): pl.pallas_call(kernel, out_shape=held, in_specs=[vmem] * 7 + [hbm] * 6, o...  61.1 us
    pallas_call x1, Pallas kernels, body(): pl.pallas_call(hand_over, out_shape=shapes, in_specs=[vmem] * 5, out_spec...  1.27 us

profile of v3, /device:TPU:1, one launch (start us, length us, event | category | flops | bytes accessed | tf_op | source)
XLA Modules:
  0.0 63.0 jit_solution(2508498710088720054)
XLA Ops:
  0.6 61.1 %shard_map.164 = (bf16[128,512]{1,0:T(8,128)(2,1)S(1)}, bf16[768,512]{1,0:T(8,128)(2,1)S(1)}, bf16[128,512]{1,0:T(8,128)(2,1)S(1)}, bf16[768,512]{1,0:T(8,128)(2,1)S(1)}, f32[56,128]{1,0:T(8,128)S(1)}) custom-call(bf16[128,512]{1,0:T(8,128)(2,1)} %tile_ref.1, s32[1,128]{1,0:T(1,128)} %pick_ref.1, s32[1,128]{1,0:T(1,128)} %bitcast.5, s32[1,32]{1,0:T(1,128)} %cut_ref.1, ...), custom_call_target="tpu_custom_call" | custom-call | tf_op jit(solution)/shard_map/pallas_call | solution.py:560
  61.8 1.3 %shard_map.165 = (bf16[128,512]{1,0:T(8,128)(2,1)}, bf16[768,512]{1,0:T(8,128)(2,1)}, bf16[128,512]{1,0:T(8,128)(2,1)}, bf16[768,512]{1,0:T(8,128)(2,1)}, f32[56,128]{1,0:T(8,128)}) custom-call(bf16[128,512]{1,0:T(8,128)(2,1)S(1)} %get-tuple-element.10.refs_0_, bf16[768,512]{1,0:T(8,128)(2,1)S(1)} %get-tuple-element.11.refs_1_, ...), custom_call_target="tpu_custom_call" | custom-call | tf_op jit(solution)/shard_map/pallas_call | solution.py:574

commit v4 on v3

--- a/solution.py
+++ b/solution.py
@@ -67,10 +67,11 @@
 
 
 def kernel(
-    tile_ref, pick_ref, from_ref, cut_ref, snd_ref, rcv_ref, ncot_ref,
+    tile_hbm, pick_hbm, from_hbm, cut_ref, snd_hbm, rcv_hbm, ncot_hbm,
     e_hbm, cot_hbm, ein_hbm, eout_hbm, nin_hbm, nout_hbm,
     nodeup_ref, enew, latgrad_ref, egrad, wgrad_ref,
-    e, cot, ein, eout, nin, nout, lsem,
+    e, cot, ein, eout, nin, nout, tile_ref, pick_ref, from_ref, snd_ref, rcv_ref, ncot_ref, lsem,
+    nbase,
     msg, inc, msgb, incb, table, lat, halo_s,
     sel_s, sel_st, sel_r, sel_rt, gat_i, back_o, back_p,
     pre, act, dsilu, normed, einv, plg, ppg,
@@ -96,6 +97,18 @@
             src, dst, ss, rs, device_id=(d, t), device_id_type=MESH
         )
 
+    first = [
+        pltpu.make_async_copy(s, d, lsem.at[6 + i])
+        for i, (s, d) in enumerate(
+            (
+                (tile_hbm, tile_ref), (pick_hbm, pick_ref), (from_hbm, from_ref),
+                (snd_hbm, snd_ref), (rcv_hbm, rcv_ref), (ncot_hbm, ncot_ref),
+            )
+        )
+    ]
+    for c in first:
+        c.start()
+
     barrier = pltpu.get_barrier_semaphore()
 
     def greet(i, carry):
@@ -120,6 +133,8 @@
     for c in loads:
         c.start()
 
+    first[0].wait()
+    first[1].wait()
     pickb = jnp.broadcast_to(pick_ref[...], (ND, LN)).astype(F32).astype(BF16)
     quad = onehot(iota((4 * LN, LN), 0) // 4 == iota((4 * LN, LN), 1))
     rep = dot_nt(quad, pickb)
@@ -155,6 +170,8 @@
 
     exchange(msg, inc, r_s, r_r)
 
+    for c in first[2:]:
+        c.wait()
     frow = jnp.broadcast_to(from_ref[...], (LN, ND))
     fcol = frow.T
     fcol4 = jnp.concatenate([fcol] * 4, 1)
@@ -212,9 +229,20 @@
     own_rows = pl.ds(pl.multiple_of(x * ND, ND), ND)
     table[own_rows, :] = latent
 
+    half_rows = ND // 2
+
+    def piece(t, part):
+        return table.at[pl.ds(pl.multiple_of(t * ND + part * half_rows, half_rows), half_rows)]
+
+    def gather_copy(t, part, j, i):
+        return remote(piece(t, part), piece(t, part), a_s.at[i], a_r.at[i], p, xpeer(j))
+
+    def arrived(t, part, i):
+        pltpu.make_async_copy(piece(t, part), piece(t, part), a_r.at[i]).wait()
+
     gathers = [
-        remote(table.at[own_rows], table.at[own_rows], a_s.at[j], a_r.at[j], p, xpeer(j))
-        for j in (1, 3, 2)
+        gather_copy(x, 0, 1, 0), gather_copy(x, 1, 3, 2),
+        gather_copy(x, 1, 1, 1), gather_copy(x, 0, 3, 3),
     ]
     for c in gathers:
         c.start()
@@ -223,8 +251,8 @@
     ccol = dot_nt(eye, cutb)
     halo_s[...] = dot(onehot(ccol == iota((32, LN), 1).astype(F32)), latent).astype(BF16)
     halos = [
-        remote(halo_s.at[pl.ds(16, 16)], table.at[pl.ds(512, 16)], a_s.at[0], a_r.at[0], up, x),
-        remote(halo_s.at[pl.ds(0, 16)], table.at[pl.ds(528, 16)], a_s.at[4], a_r.at[4], dn, x),
+        remote(halo_s.at[pl.ds(16, 16)], table.at[pl.ds(512, 16)], a_s.at[6], a_r.at[6], up, x),
+        remote(halo_s.at[pl.ds(0, 16)], table.at[pl.ds(528, 16)], a_s.at[7], a_r.at[7], dn, x),
     ]
     for c in halos:
         c.start()
@@ -248,9 +276,18 @@
         back_p[:, c * ND : (c + 1) * ND] = onehot((frow4 - ND) * 4 + c == fq)
     for c in loads[2:]:
         c.wait()
-
-    for c in gathers:
-        c.wait_recv()
+    nbase[...] = dot(latent, nin[:H, :])
+
+    arrived(xpeer(3), 0, 0)
+    forwards = [gather_copy(xpeer(3), 0, 1, 4)]
+    forwards[0].start()
+    arrived(xpeer(1), 1, 2)
+    forwards.append(gather_copy(xpeer(1), 1, 3, 5))
+    forwards[1].start()
+    arrived(xpeer(3), 1, 1)
+    arrived(xpeer(1), 0, 3)
+    arrived(xpeer(2), 0, 4)
+    arrived(xpeer(2), 1, 5)
     for c in halos:
         c.wait_recv()
 
@@ -270,7 +307,7 @@
     lax.fori_loop(0, ED // EF, edge_forward, 0)
 
     agg = dot(sel_rt[...], enew[...]).astype(BF16)
-    node_act, node_dsilu = silu_pair(dot(latent, nin[:H, :]) + dot(agg, nin[H:, :]))
+    node_act, node_dsilu = silu_pair(nbase[...] + dot(agg, nin[H:, :]))
     node_act = node_act.astype(BF16)
     nnorm, ninv = norm(dot(node_act, nout[...]))
     nodeup_ref[...] = (latent.astype(F32) + nnorm).astype(BF16)
@@ -279,7 +316,6 @@
     npg = (dot_nt(nlg, nout[...]) * node_dsilu).astype(BF16)
     agh, agl = hi_lo(dot_nt(npg, nin[H:, :]))
     agg_grad = jnp.concatenate([agh, agl], 0)
-    node_direct = ncot + dot_nt(npg, nin[:H, :])
     wg[4 * H : 5 * H, :] = dot_tn(latent, npg)
     wg[5 * H : 6 * H, :] = dot_tn(agg, npg)
     wg[6 * H :, :] = dot_tn(node_act, nlg)
@@ -384,16 +420,12 @@
         plg[rows, :] = g
         pg = (dot_nt(g, eout[...]) * dsilu[rows, :]).astype(BF16)
         ppg[rows, :] = pg
-        egrad[rows, :] = (upst + dot_nt(pg, ein[:H, :])).astype(BF16)
         return carry
 
     lax.fori_loop(0, 1, edge_backward, 0)
     for block in (7, 6, 5):
         combine(block)
     lax.fori_loop(1, ED // EB, edge_backward, 0)
-    gsum[...] = dot(sel_st[...], ppg[...])
-    gs[...] = gsum[...].astype(BF16)
-
     def own_of(t):
         return pl.ds(pl.multiple_of(t * ND, ND), ND)
 
@@ -404,21 +436,32 @@
         remote(gs.at[pl.ds(512, 16)], hb.at[pl.ds(16, 16)], g_s.at[0], g_r.at[0], dn, x),
         remote(gs.at[pl.ds(528, 16)], hb.at[pl.ds(0, 16)], g_s.at[4], g_r.at[4], up, x),
     ]
+    wg[:H, :] = dot_tn(e[...], ppg[...])
+    pack_core(0)
+    grecv = dot(sel_rt[...], ppg[...]).astype(BF16)
+    wg[2 * H : 3 * H, :] = dot_tn(latent, grecv)
+    gsum[...] = dot(sel_st[...], ppg[...])
+    gs[...] = gsum[...].astype(BF16)
+    wg[H : 2 * H, :] = dot_tn(table[...], gs[...])
+    pack_core(2)
+    pack_core(1)
+    wg[3 * H : 4 * H, :] = dot_tn(act[...], plg[...])
+    pack_core(3)
+    pack_core(4)
     for c in scatters:
         c.start()
-    wg[3 * H : 4 * H, :] = dot_tn(act[...], plg[...])
-    grecv = dot(sel_rt[...], ppg[...]).astype(BF16)
-    wg[2 * H : 3 * H, :] = dot_tn(latent, grecv)
-    pack_core(3)
-    wg[H : 2 * H, :] = dot_tn(table[...], gs[...])
-    wg[:H, :] = dot_tn(e[...], ppg[...])
-    for block in (1, 2, 0, 4):
-        pack_core(block)
+    for block in (0, 2, 1, 3, 4):
+        combine(block)
+
+    def edge_result(b, carry):
+        rows = pl.ds(pl.multiple_of(b * EB, EB), EB)
+        total = cot[rows, :].astype(F32) + dot(sel_r[rows, :], agg_grad)
+        egrad[rows, :] = (total + dot_nt(ppg[rows, :], ein[:H, :])).astype(BF16)
+        return carry
+
+    lax.fori_loop(0, ED // EB, edge_result, 0)
+    node_direct = ncot + dot_nt(npg, nin[:H, :])
     node_part = node_direct + dot_nt(grecv, ein[2 * H :, :])
-    for block in (3, 1, 2, 0, 4):
-        combine(block)
-    for block in (7, 6, 5):
-        finish_x(block)
 
     for c in scatters:
         c.wait_recv()
@@ -432,6 +475,8 @@
     msgb[...] = dot(back_p[...], ng).reshape(DOM, 8, LN).astype(BF16)
 
     exchange(msgb, incb, rb_s, rb_r)
+    for block in (7, 6, 5):
+        finish_x(block)
 
     def z_copy(t):
         i = lax.rem(t - z + NZ, NZ) - 1
@@ -459,14 +504,14 @@
             def _():
                 z_copy(t).start()
 
-    for block in (3, 1):
+    for block in (0, 2):
+        finish_x(block)
+    finish_y(0)
+    for block in (1, 3, 4):
         finish_x(block)
     finish_y(1)
-    for block in (4, 2, 0):
-        finish_x(block)
-    finish_y(0)
+    half_sum(0)
     half_sum(1)
-    half_sum(0)
 
     pltpu.make_async_copy(incb.at[pl.ds(0, DOM - 1)], incb.at[pl.ds(0, DOM - 1)], rb_r).wait()
     back = incb[...].astype(F32).reshape(4 * LN, LN).astype(BF16)
@@ -491,7 +536,7 @@
 
     pltpu.make_async_copy(msg.at[pl.ds(0, DOM - 1)], msg.at[pl.ds(0, DOM - 1)], r_s).wait()
     pltpu.make_async_copy(msgb.at[pl.ds(0, DOM - 1)], msgb.at[pl.ds(0, DOM - 1)], rb_s).wait()
-    for c in gathers + halos + scatters:
+    for c in gathers + forwards + halos + scatters:
         c.wait_send()
     for block in range(8):
         core_copy(block).wait_send()
@@ -524,11 +569,14 @@
 ):
     vmem = pl.BlockSpec(memory_space=pltpu.VMEM)
     hbm = pl.BlockSpec(memory_space=pl.ANY)
+    pin = pl.BlockSpec(memory_space=pltpu.HBM)
     dma = pltpu.SemaphoreType.DMA
     V = pltpu.VMEM
     scratch = [
         V((ED, H), BF16), V((ED, H), BF16), V((3 * H, H), BF16), V((H, H), BF16),
-        V((2 * H, H), BF16), V((H, H), BF16), dma((8,)),
+        V((2 * H, H), BF16), V((H, H), BF16), V((ND, H), BF16), V((1, LN), jnp.int32),
+        V((1, ND), jnp.int32), V((ED // LN, LN), jnp.int32), V((ED // LN, LN), jnp.int32),
+        V((ND, H), BF16), dma((12,)), V((ND, H), F32),
         V((DOM, 8, LN), BF16), V((DOM, 8, LN), BF16), V((DOM, 8, LN), BF16), V((DOM, 8, LN), BF16),
         V((TR, H), BF16), V((ND, H), BF16), V((32, H), BF16),
         V((ED, TR), BF16), V((TR, ED), BF16), V((ED, 2 * LN), BF16), V((ND, ED), BF16),
@@ -540,7 +588,7 @@
         V((24, RX, LN), BF16), V((8, RX, LN), BF16), V((6, RX, LN), BF16),
         V((6, RY, H), BF16), V((2, RY, H), BF16), V((6, RY, LN), BF16),
         V((2 * SUB, LN), F32), V((NZ, 64, LN), BF16), V((NZ - 1, 64, LN), BF16),
-        dma, dma, dma((5,)), dma((5,)), dma, dma, dma((5,)), dma((5,)), dma((8,)), dma((8,)),
+        dma, dma, dma((8,)), dma((8,)), dma, dma, dma((5,)), dma((5,)), dma((8,)), dma((8,)),
         dma((24,)), dma((24,)), dma((6,)), dma((6,)), dma((6,)), dma((6,)), dma((6,)), dma((6,)),
         dma((NZ - 1,)), dma((NZ - 1,)),
     ]
@@ -560,7 +608,7 @@
     parts = pl.pallas_call(
         kernel,
         out_shape=held,
-        in_specs=[vmem] * 7 + [hbm] * 6,
+        in_specs=[pin] * 3 + [vmem] + [pin] * 3 + [hbm] * 6,
         out_specs=(vmem,) * 5,
         scratch_shapes=scratch,
         compiler_params=pltpu.CompilerParams(

time: 63.4 us -> 60.7 us (0.957)
  Pallas kernels: 62.4 us -> 59.7 us
    pallas_call x1, Pallas kernels: 61.1 us -> 58.5 us  [body(): pl.pallas_call(kernel, out_shape=held, in_specs=[pin] * 3 + [vmem] + [pin...]
where the time goes in v4:
time: 60.7 us; the launch traced here: 60.4 us
  Pallas kernels  59.7 us (98%)
  between operations  0.64 us (1%)
    pallas_call x1, Pallas kernels, body(): pl.pallas_call(kernel, out_shape=held, in_specs=[pin] * 3 + [vmem] + [pin...  58.5 us
    pallas_call x1, Pallas kernels, body(): pl.pallas_call(hand_over, out_shape=shapes, in_specs=[vmem] * 5, out_spec...  1.27 us

profile of v4, /device:TPU:1, one launch (start us, length us, event | category | flops | bytes accessed | tf_op | source)
XLA Modules:
  0.0 60.4 jit_solution(4791198600504976250)
XLA Ops:
  0.6 58.5 %shard_map.164 = (bf16[128,512]{1,0:T(8,128)(2,1)S(1)}, bf16[768,512]{1,0:T(8,128)(2,1)S(1)}, bf16[128,512]{1,0:T(8,128)(2,1)S(1)}, bf16[768,512]{1,0:T(8,128)(2,1)S(1)}, f32[56,128]{1,0:T(8,128)S(1)}) custom-call(bf16[128,512]{1,0:T(8,128)(2,1)} %tile_hbm.1, s32[1,128]{1,0:T(1,128)} %pick_hbm.1, s32[1,128]{1,0:T(1,128)} %bitcast.5, s32[1,32]{1,0:T(1,128)} %cut_ref.1, ...), custom_call_target="tpu_custom_call" | custom-call | tf_op jit(solution)/shard_map/pallas_call | solution.py:608
  59.1 1.3 %shard_map.165 = (bf16[128,512]{1,0:T(8,128)(2,1)}, bf16[768,512]{1,0:T(8,128)(2,1)}, bf16[128,512]{1,0:T(8,128)(2,1)}, bf16[768,512]{1,0:T(8,128)(2,1)}, f32[56,128]{1,0:T(8,128)}) custom-call(bf16[128,512]{1,0:T(8,128)(2,1)S(1)} %get-tuple-element.10.refs_0_, bf16[768,512]{1,0:T(8,128)(2,1)S(1)} %get-tuple-element.11.refs_1_, ...), custom_call_target="tpu_custom_call" | custom-call | tf_op jit(solution)/shard_map/pallas_call | solution.py:622

commit v5 on v4

--- a/solution.py
+++ b/solution.py
@@ -422,10 +422,7 @@
         ppg[rows, :] = pg
         return carry
 
-    lax.fori_loop(0, 1, edge_backward, 0)
-    for block in (7, 6, 5):
-        combine(block)
-    lax.fori_loop(1, ED // EB, edge_backward, 0)
+    lax.fori_loop(0, ED // EB, edge_backward, 0)
     def own_of(t):
         return pl.ds(pl.multiple_of(t * ND, ND), ND)
 
@@ -438,6 +435,8 @@
     ]
     wg[:H, :] = dot_tn(e[...], ppg[...])
     pack_core(0)
+    for block in (7, 6, 5):
+        combine(block)
     grecv = dot(sel_rt[...], ppg[...]).astype(BF16)
     wg[2 * H : 3 * H, :] = dot_tn(latent, grecv)
     gsum[...] = dot(sel_st[...], ppg[...])

time: 60.7 us -> 61.3 us (level)
  the two profiles are of different devices: /device:TPU:1 before, /device:TPU:16 now
where the time goes in v5:
time: 61.3 us; the launch traced here: 61.1 us
  Pallas kernels  60.5 us (99%)
  between operations  0.64 us (1%)
    pallas_call x1, Pallas kernels, body(): pl.pallas_call(kernel, out_shape=held, in_specs=[pin] * 3 + [vmem] + [pin...  59.2 us
    pallas_call x1, Pallas kernels, body(): pl.pallas_call(hand_over, out_shape=shapes, in_specs=[vmem] * 5, out_spec...  1.27 us

profile of v5, /device:TPU:16, one launch (start us, length us, event | category | flops | bytes accessed | tf_op | source)
XLA Modules:
  0.0 61.1 jit_solution(9243969482715900221)
XLA Ops:
  0.6 59.2 %shard_map.164 = (bf16[128,512]{1,0:T(8,128)(2,1)S(1)}, bf16[768,512]{1,0:T(8,128)(2,1)S(1)}, bf16[128,512]{1,0:T(8,128)(2,1)S(1)}, bf16[768,512]{1,0:T(8,128)(2,1)S(1)}, f32[56,128]{1,0:T(8,128)S(1)}) custom-call(bf16[128,512]{1,0:T(8,128)(2,1)} %tile_hbm.1, s32[1,128]{1,0:T(1,128)} %pick_hbm.1, s32[1,128]{1,0:T(1,128)} %bitcast.5, s32[1,32]{1,0:T(1,128)} %cut_ref.1, ...), custom_call_target="tpu_custom_call" | custom-call | tf_op jit(solution)/shard_map/pallas_call | solution.py:607
  59.9 1.3 %shard_map.165 = (bf16[128,512]{1,0:T(8,128)(2,1)}, bf16[768,512]{1,0:T(8,128)(2,1)}, bf16[128,512]{1,0:T(8,128)(2,1)}, bf16[768,512]{1,0:T(8,128)(2,1)}, f32[56,128]{1,0:T(8,128)}) custom-call(bf16[128,512]{1,0:T(8,128)(2,1)S(1)} %get-tuple-element.10.refs_0_, bf16[768,512]{1,0:T(8,128)(2,1)S(1)} %get-tuple-element.11.refs_1_, ...), custom_call_target="tpu_custom_call" | custom-call | tf_op jit(solution)/shard_map/pallas_call | solution.py:621
